TPU v7x, 32 devices: a whole 2x2x4 slice. The times are simulated.
32 devices in a mesh: section: 2 (over x), dp: 16 (over z, y, core).
Axes of the slice: x: 2, y: 2, z: 4, core: 2. Of those that a mesh axis runs over, the one named last changes fastest.
Arguments:
- tokens: bfloat16 [2, 16, 384, 768], P('section', 'dp'), may hold values from -6 to 6
- segments: int32 [2, 16, 384], P(None, 'dp'), may hold values from 0 to 6, as said below
- cotangent: bfloat16 [16, 384, 768], P('dp'), may hold values from -6 to 6
- attn_qk: bfloat16 [2, 768, 1536], P('section', 'dp'), may hold values from -0.21875 to 0.21875
- attn_vo: bfloat16 [2, 768, 1536], P('section', 'dp'), may hold values from -0.625 to 0.625
- cross_qk: bfloat16 [2, 768, 768], P('section', 'dp'), may hold values from -0.21875 to 0.21875
- cross_vo: bfloat16 [2, 768, 768], P('section', 'dp'), may hold values from -0.625 to 0.625
- ffn_in: bfloat16 [2, 768, 3072], P('section', 'dp'), may hold values from -0.21875 to 0.21875
- ffn_out: bfloat16 [2, 3072, 768], P('section', 'dp'), may hold values from -0.109375 to 0.109375
- gains: float32 [5, 768], replicated, may hold values from 0.5 to 1.5
- biases: float32 [16, 768], replicated, may hold values from -1.25 to 1.25
- ffn_bias: float32 [2, 3072], replicated, may hold values from -1.25 to 1.25
Outputs:
- layer_out: bfloat16 [2, 16, 384, 768], P('section', 'dp')
- input_grad: float32 [2, 16, 384, 768], P('section', 'dp')
- grad_attn_qk: float32 [2, 768, 1536], P('section', 'dp')
- grad_attn_vo: float32 [2, 768, 1536], P('section', 'dp')
- grad_cross_qk: float32 [2, 768, 768], P('section', 'dp')
- grad_cross_vo: float32 [2, 768, 768], P('section', 'dp')
- grad_ffn_in: float32 [2, 768, 3072], P('section', 'dp')
- grad_ffn_out: float32 [2, 3072, 768], P('section', 'dp')
- grad_gains: float32 [5, 768], replicated
- grad_biases: float32 [16, 768], replicated
- grad_ffn_bias: float32 [2, 3072], replicated
Inputs may be any that keep to these rules, and one draw needn't show every extreme that they name: `segments`: in each row, ids 1 to n (2 <= n <= 6) fill runs of consecutive tokens in increasing order, followed by one or more padding tokens of id 0; the source row and the target row of the same index hold the same ids, with their own lengths; row 0 holds 6 documents.
All inputs are finite; a program needn't handle non-finite values.
Results may differ from a plain program's by a relative error of at most 0.025.
Values may be sent and summed in bfloat16 or wider, within the bound.
A program may use at most 192 MiB of HBM per device.

v0:
```python
import jax
import jax.numpy as jnp
from jax import lax
from jax.sharding import PartitionSpec as P

HEADS = 12


NORM_EPSILON = 1e-05


def from_behind(x, axis, by):
    devices = lax.axis_size(axis)
    pairs = [(i, i + by) for i in range(devices) if 0 <= i + by < devices]
    return lax.ppermute(x, axis, pairs)


def product(left, right):
    return jnp.einsum("rld,de->rle", left, right, preferred_element_type=jnp.float32)


def back_product(grad, right):
    return jnp.einsum("rle,de->rld", grad, right, preferred_element_type=jnp.float32)


def weight_grad(left, grad):
    return jnp.einsum("rld,rle->de", left, grad, preferred_element_type=jnp.float32)


def column_sum(values):
    return jnp.sum(values.astype(jnp.float32), axis=(0, 1))


def norm_rows(resid, gain, shift):
    center = resid - jnp.mean(resid, axis=-1, keepdims=True)
    spread = jnp.mean(center * center, axis=-1, keepdims=True)
    return center * lax.rsqrt(spread + NORM_EPSILON) * gain + shift


def norm_back(resid, gain, shift, grad):
    unused, pull = jax.vjp(norm_rows, resid, gain, shift)
    return pull(grad)


def split_heads(values, head_count):
    return values.reshape(
        values.shape[0], values.shape[1], head_count, values.shape[2] // head_count
    )


def masked_scores(query_heads, key_heads, allowed):
    scale = query_heads.shape[-1] ** (-0.5)
    scores = (
        jnp.einsum("rqhe,rkhe->rhqk", query_heads, key_heads, preferred_element_type=jnp.float32)
        * scale
    )
    return jnp.where(allowed[:, None], scores, -1e30)


def attend(query, key_rows, value_rows, allowed, head_count):
    query_heads = split_heads(query, head_count)
    scores = masked_scores(query_heads, split_heads(key_rows, head_count), allowed)
    peak = jnp.max(scores, axis=-1, keepdims=True)
    exponent = jnp.exp(scores - peak)
    summed = jnp.sum(exponent, axis=-1, keepdims=True)
    soft = (exponent / summed).astype(jnp.bfloat16)
    mixed = jnp.einsum(
        "rhqk,rkhe->rqhe",
        soft,
        split_heads(value_rows, head_count),
        preferred_element_type=jnp.float32,
    )
    return (mixed.reshape(query.shape), peak + jnp.log(summed))


def attend_back(query, key_rows, value_rows, allowed, log_total, grad_mixed, head_count):
    query_heads = split_heads(query, head_count)
    key_heads = split_heads(key_rows, head_count)
    value_heads = split_heads(value_rows, head_count)
    grad_heads = split_heads(grad_mixed, head_count)
    scale = query_heads.shape[-1] ** (-0.5)
    soft = jnp.exp(masked_scores(query_heads, key_heads, allowed) - log_total)
    grad_values = jnp.einsum(
        "rhqk,rqhe->rkhe", soft.astype(jnp.bfloat16), grad_heads, preferred_element_type=jnp.float32
    )
    grad_soft = jnp.einsum(
        "rqhe,rkhe->rhqk", grad_heads, value_heads, preferred_element_type=jnp.float32
    )
    inner_sum = jnp.sum(soft * grad_soft, axis=-1, keepdims=True)
    grad_scores = (soft * (grad_soft - inner_sum)).astype(jnp.bfloat16)
    grad_query = (
        jnp.einsum("rhqk,rkhe->rqhe", grad_scores, key_heads, preferred_element_type=jnp.float32)
        * scale
    )
    grad_keys = (
        jnp.einsum("rhqk,rqhe->rkhe", grad_scores, query_heads, preferred_element_type=jnp.float32)
        * scale
    )
    return (
        grad_query.reshape(query.shape),
        grad_keys.reshape(key_rows.shape),
        grad_values.reshape(key_rows.shape),
    )


def self_forward(inputs, w_qk, w_vo, section_bias, gain, allowed, head_count):
    model_width = inputs.shape[-1]
    query = (product(inputs, w_qk[:, :model_width]) + section_bias[0]).astype(jnp.bfloat16)
    key_rows = product(inputs, w_qk[:, model_width:]).astype(jnp.bfloat16)
    value_rows = (product(inputs, w_vo[:, :model_width]) + section_bias[1]).astype(jnp.bfloat16)
    mixed, log_total = attend(query, key_rows, value_rows, allowed, head_count)
    mixed = mixed.astype(jnp.bfloat16)
    resid = inputs.astype(jnp.float32) + product(mixed, w_vo[:, model_width:]) + section_bias[2]
    return (
        norm_rows(resid, gain, section_bias[3]),
        (query, key_rows, value_rows, log_total, mixed, resid),
    )


def self_backward(inputs, w_qk, w_vo, section_bias, gain, allowed, head_count, kept, grad_hidden):
    query, key_rows, value_rows, log_total, mixed, resid = kept
    model_width = inputs.shape[-1]
    grad_resid, grad_gain, grad_shift = norm_back(resid, gain, section_bias[3], grad_hidden)
    grad_branch = grad_resid.astype(jnp.bfloat16)
    grad_mixed = back_product(grad_branch, w_vo[:, model_width:]).astype(jnp.bfloat16)
    grad_query, grad_keys, grad_values = attend_back(
        query, key_rows, value_rows, allowed, log_total, grad_mixed, head_count
    )
    grad_query = grad_query.astype(jnp.bfloat16)
    grad_keys = grad_keys.astype(jnp.bfloat16)
    grad_values = grad_values.astype(jnp.bfloat16)
    grad_pair = jnp.concatenate([grad_query, grad_keys], axis=-1)
    grad_inputs = (
        grad_resid
        + back_product(grad_pair, w_qk)
        + back_product(grad_values, w_vo[:, :model_width])
    )
    grad_rows = jnp.stack(
        [column_sum(grad_query), column_sum(grad_values), column_sum(grad_branch), grad_shift]
    )
    return (grad_inputs, (inputs, grad_pair, grad_values, mixed, grad_branch), grad_rows, grad_gain)


def ffn_forward(hidden, w_in, w_out, b_in, b_out):
    hidden_low = hidden.astype(jnp.bfloat16)
    pre_act = product(hidden_low, w_in) + b_in
    activated = jax.nn.gelu(pre_act, approximate=False).astype(jnp.bfloat16)
    return (product(activated, w_out) + b_out, (hidden_low, pre_act, activated))


def gelu_exact(values):
    return jax.nn.gelu(values, approximate=False)


def ffn_backward(w_in, w_out, kept, grad_branch):
    hidden_low, pre_act, activated = kept
    grad_low = grad_branch.astype(jnp.bfloat16)
    grad_act = back_product(grad_low, w_out)
    unused, pull = jax.vjp(gelu_exact, pre_act)
    grad_pre = pull(grad_act)[0].astype(jnp.bfloat16)
    grad_hidden = back_product(grad_pre, w_in)
    return (
        grad_hidden,
        (hidden_low, grad_pre, activated, grad_low),
        column_sum(grad_pre),
        column_sum(grad_low),
    )


def encoder_forward(hidden, w_in, w_out, b_in, section_bias, gain_last, w_ck, w_cv, bias_cv):
    branch, kept = ffn_forward(hidden, w_in, w_out, b_in, section_bias[4])
    resid = hidden + branch
    memory = norm_rows(resid, gain_last, section_bias[5]).astype(jnp.bfloat16)
    key_rows = product(memory, w_ck).astype(jnp.bfloat16)
    value_rows = (product(memory, w_cv) + bias_cv).astype(jnp.bfloat16)
    return (memory, key_rows, value_rows, resid, kept)


def encoder_backward(
    w_in, w_out, section_bias, gain_last, w_ck, w_cv, memory, resid, kept, grad_keys, grad_values
):
    grad_memory = back_product(grad_keys, w_ck) + back_product(grad_values, w_cv)
    grad_last, grad_gain, grad_shift = norm_back(resid, gain_last, section_bias[5], grad_memory)
    grad_ffn, ffn_ops, grad_bin, grad_bout = ffn_backward(w_in, w_out, kept, grad_last)
    zero_line = jnp.zeros_like(grad_gain)
    cross_rows = jnp.stack([zero_line, column_sum(grad_values), zero_line, zero_line])
    operands = (memory, grad_keys, memory, grad_values) + ffn_ops
    return (
        grad_last + grad_ffn,
        operands,
        grad_bin,
        grad_bout,
        grad_gain,
        grad_shift,
        cross_rows,
        zero_line,
    )


def decoder_step(
    hidden,
    w_cq,
    w_co,
    w_in,
    w_out,
    b_in,
    section_bias,
    gain_last,
    gain_cross,
    cross_bias,
    key_rows,
    value_rows,
    allowed,
    cotangent,
    head_count,
):
    hidden_low = hidden.astype(jnp.bfloat16)
    query = (product(hidden_low, w_cq) + cross_bias[0]).astype(jnp.bfloat16)
    mixed, log_total = attend(query, key_rows, value_rows, allowed, head_count)
    mixed = mixed.astype(jnp.bfloat16)
    resid_mid = hidden + product(mixed, w_co) + cross_bias[2]
    middle = norm_rows(resid_mid, gain_cross, cross_bias[3])
    branch, kept = ffn_forward(middle, w_in, w_out, b_in, section_bias[4])
    resid_last = middle + branch
    result = norm_rows(resid_last, gain_last, section_bias[5])
    grad_last, grad_gain, grad_shift = norm_back(
        resid_last, gain_last, section_bias[5], cotangent.astype(jnp.float32)
    )
    grad_ffn, ffn_ops, grad_bin, grad_bout = ffn_backward(w_in, w_out, kept, grad_last)
    grad_mid, grad_gain_cross, grad_shift_cross = norm_back(
        resid_mid, gain_cross, cross_bias[3], grad_last + grad_ffn
    )
    grad_branch = grad_mid.astype(jnp.bfloat16)
    grad_mixed = back_product(grad_branch, w_co).astype(jnp.bfloat16)
    grad_query, grad_keys, grad_values = attend_back(
        query, key_rows, value_rows, allowed, log_total, grad_mixed, head_count
    )
    grad_query = grad_query.astype(jnp.bfloat16)
    grad_hidden = grad_mid + back_product(grad_query, w_cq)
    cross_rows = jnp.stack(
        [
            column_sum(grad_query),
            jnp.zeros_like(grad_gain),
            column_sum(grad_branch),
            grad_shift_cross,
        ]
    )
    operands = (hidden_low, grad_query, mixed, grad_branch) + ffn_ops
    tail_result = (
        grad_hidden,
        operands,
        grad_bin,
        grad_bout,
        grad_gain,
        grad_shift,
        cross_rows,
        grad_gain_cross,
    )
    return (
        result.astype(jnp.bfloat16),
        grad_keys.astype(jnp.bfloat16),
        grad_values.astype(jnp.bfloat16),
        tail_result,
    )


def zero_tail(hidden, w_in):
    model_width = hidden.shape[-1]
    ffn_width = w_in.shape[1]
    flat = jnp.zeros(hidden.shape, jnp.bfloat16)
    wide = jnp.zeros((hidden.shape[0], hidden.shape[1], ffn_width), jnp.bfloat16)
    zero_line = jnp.zeros((model_width,), jnp.float32)
    operands = (flat, flat, flat, flat, flat, wide, wide, flat)
    return (
        jnp.zeros_like(hidden),
        operands,
        jnp.zeros((ffn_width,), jnp.float32),
        zero_line,
        zero_line,
        zero_line,
        jnp.zeros((4, model_width), jnp.float32),
        zero_line,
    )


def tail_whole(operands):
    return (
        weight_grad(operands[0], operands[1]),
        weight_grad(operands[2], operands[3]),
        weight_grad(operands[4], operands[5]),
        weight_grad(operands[6], operands[7]),
    )


def self_whole(operands):
    grad_qk = weight_grad(operands[0], operands[1])
    grad_vo = jnp.concatenate(
        [weight_grad(operands[0], operands[2]), weight_grad(operands[3], operands[4])], axis=1
    )
    return (grad_qk, grad_vo)


def local(
    tokens,
    segments,
    cotangent,
    attn_qk,
    attn_vo,
    cross_qk,
    cross_vo,
    ffn_in,
    ffn_out,
    gains,
    biases,
    ffn_bias,
):
    head_count = HEADS
    section_index = lax.axis_index("section")
    is_enc = section_index == 0
    qk_whole, vo_whole = (
        lax.all_gather(attn_qk, "dp", axis=1, tiled=True),
        lax.all_gather(attn_vo, "dp", axis=1, tiled=True),
    )
    w_qk = qk_whole[0]
    w_vo = vo_whole[0]
    cqk_whole, cvo_whole, in_whole, out_whole = (
        lax.all_gather(cross_qk, "dp", axis=1, tiled=True),
        lax.all_gather(cross_vo, "dp", axis=1, tiled=True),
        lax.all_gather(ffn_in, "dp", axis=1, tiled=True),
        lax.all_gather(ffn_out, "dp", axis=1, tiled=True),
    )
    w_cqk = cqk_whole[0]
    w_cvo = cvo_whole[0]
    w_in = in_whole[0]
    w_out = out_whole[0]
    section_bias = lax.dynamic_slice_in_dim(biases, 6 * section_index, 6, 0)
    section_gain = lax.dynamic_slice_in_dim(gains, 2 * section_index, 2, 0)
    bias_in = lax.dynamic_index_in_dim(ffn_bias, section_index, 0, keepdims=False)
    section_seg = lax.dynamic_index_in_dim(segments, section_index, 0, keepdims=False)
    length = tokens.shape[2]
    position = jnp.arange(length)
    earlier = position[None, :] <= position[:, None]
    allowed_self = (section_seg[:, :, None] == section_seg[:, None, :]) & (earlier[None] | is_enc)
    allowed_cross = segments[1][:, :, None] == segments[0][:, None, :]
    source = tokens[0]
    hidden_one, kept_self = self_forward(
        source, w_qk, w_vo, section_bias, section_gain[0], allowed_self, head_count
    )

    def run_encoder():
        return encoder_forward(
            hidden_one,
            w_in,
            w_out,
            bias_in,
            section_bias,
            section_gain[1],
            w_cqk,
            w_cvo,
            biases[13],
        )

    def skip_encoder():
        flat = jnp.zeros(hidden_one.shape, jnp.bfloat16)
        wide_shape = (hidden_one.shape[0], hidden_one.shape[1], w_in.shape[1])
        return (
            flat,
            flat,
            flat,
            jnp.zeros_like(hidden_one),
            (flat, jnp.zeros(wide_shape, jnp.float32), jnp.zeros(wide_shape, jnp.bfloat16)),
        )

    memory, enc_keys, enc_values, enc_resid, enc_kept = lax.cond(is_enc, run_encoder, skip_encoder)
    got_keys, got_values = from_behind((enc_keys, enc_values), "section", 1)

    def run_decoder():
        return decoder_step(
            hidden_one,
            w_cqk,
            w_cvo,
            w_in,
            w_out,
            bias_in,
            section_bias,
            section_gain[1],
            gains[4],
            biases[12:16],
            got_keys,
            got_values,
            allowed_cross,
            cotangent,
            head_count,
        )

    def skip_decoder():
        flat = jnp.zeros(hidden_one.shape, jnp.bfloat16)
        return (flat, flat, flat, zero_tail(hidden_one, w_in))

    decoded, grad_keys, grad_values, dec_tail = lax.cond(is_enc, skip_decoder, run_decoder)
    back_keys, back_values = from_behind((grad_keys, grad_values), "section", -1)

    def run_encoder_back():
        return encoder_backward(
            w_in,
            w_out,
            section_bias,
            section_gain[1],
            w_cqk,
            w_cvo,
            memory,
            enc_resid,
            enc_kept,
            back_keys,
            back_values,
        )

    def keep_decoder():
        return dec_tail

    tail_result = lax.cond(is_enc, run_encoder_back, keep_decoder)
    (
        grad_hidden,
        tail_ops,
        grad_bin,
        grad_bout,
        grad_gain_last,
        grad_shift_last,
        cross_rows,
        grad_gain_cross,
    ) = tail_result
    layer_out = jnp.where(is_enc, memory, decoded)
    model_width = source.shape[-1]
    grad_ca, grad_cb, grad_in, grad_out = tail_whole(tail_ops)
    tail_parts = (
        lax.psum_scatter(grad_ca[None], "dp", scatter_dimension=1, tiled=True),
        lax.psum_scatter(grad_cb[None], "dp", scatter_dimension=1, tiled=True),
        lax.psum_scatter(grad_in[None], "dp", scatter_dimension=1, tiled=True),
        lax.psum_scatter(grad_out[None], "dp", scatter_dimension=1, tiled=True),
    )
    grad_source, self_ops, self_rows, grad_gain_first = self_backward(
        source,
        w_qk,
        w_vo,
        section_bias,
        section_gain[0],
        allowed_self,
        head_count,
        kept_self,
        grad_hidden,
    )
    grad_qk, grad_vo = self_whole(self_ops)
    attn_parts = (
        lax.psum_scatter(grad_qk[None], "dp", scatter_dimension=1, tiled=True),
        lax.psum_scatter(grad_vo[None], "dp", scatter_dimension=1, tiled=True),
    )
    large_parts = tuple(attn_parts) + tuple(tail_parts)
    section_rows = jnp.concatenate([self_rows, jnp.stack([grad_bout, grad_shift_last])], axis=0)
    bias_block = lax.dynamic_update_slice_in_dim(
        jnp.zeros((12, model_width), jnp.float32), section_rows, 6 * section_index, 0
    )
    grad_biases = jnp.concatenate([bias_block, cross_rows], axis=0)
    gain_block = lax.dynamic_update_slice_in_dim(
        jnp.zeros((4, model_width), jnp.float32),
        jnp.stack([grad_gain_first, grad_gain_last]),
        2 * section_index,
        0,
    )
    grad_gains = jnp.concatenate([gain_block, grad_gain_cross[None]], axis=0)
    grad_fbias = lax.dynamic_update_slice_in_dim(
        jnp.zeros_like(ffn_bias), grad_bin[None], section_index, 0
    )
    sum_gains, sum_biases, sum_fbias = lax.psum(
        (grad_gains, grad_biases, grad_fbias), ("section", "dp")
    )
    return (
        layer_out[None],
        grad_source[None],
        large_parts[0],
        large_parts[1],
        large_parts[2],
        large_parts[3],
        large_parts[4],
        large_parts[5],
        sum_gains,
        sum_biases,
        sum_fbias,
    )


def solution(mesh):
    placed = (
        P("section", "dp", None, None),
        P(None, "dp", None),
        P("dp", None, None),
        P("section", "dp", None),
        P("section", "dp", None),
        P("section", "dp", None),
        P("section", "dp", None),
        P("section", "dp", None),
        P("section", "dp", None),
        P(),
        P(),
        P(),
    )
    return jax.shard_map(
        local,
        mesh=mesh,
        in_specs=placed,
        out_specs=(
            P("section", "dp", None, None),
            P("section", "dp", None, None),
            P("section", "dp", None),
            P("section", "dp", None),
            P("section", "dp", None),
            P("section", "dp", None),
            P("section", "dp", None),
            P("section", "dp", None),
            P(),
            P(),
            P(),
        ),
        check_vma=False,
    )
```

profile of v0, /device:TPU:0, one launch (start us, length us, event | category | flops | bytes accessed | tf_op | source)
XLA Modules:
  0.0 1241.5 jit_solution(4260237799088343322)
XLA Ops:
  15.4 39.8 %all-gather.7.cloned.1.call-done = bf16[1,768,1536]{2,1,0:T(8,128)(2,1)} async-done(((bf16[1,48,1536]{2,1,0:T(8,128)(2,1)}), bf16[1,768,1536]{2,1,0:T(8,128)(2,1)}) %all-gather.7.cloned.1.call-update) | async-done | bytes 2359312 | tf_op jit(solution)/shard_map/all_gather | solution.py:322
  57.7 40.9 %all-gather.9.cloned.1.call-done = bf16[1,768,1536]{2,1,0:T(8,128)(2,1)} async-done(((bf16[1,48,1536]{2,1,0:T(8,128)(2,1)}), bf16[1,768,1536]{2,1,0:T(8,128)(2,1)}) %all-gather.9.cloned.1.call-update) | async-done | bytes 2359312 | tf_op jit(solution)/shard_map/all_gather | solution.py:321
  111.0 27.0 %all-gather.15.cloned.1.call-done = bf16[1,768,768]{2,1,0:T(8,128)(2,1)} async-done(((bf16[1,48,768]{2,1,0:T(8,128)(2,1)}), bf16[1,768,768]{2,1,0:T(8,128)(2,1)}) %all-gather.15.cloned.1.call-update) | async-done | bytes 1179664 | tf_op jit(solution)/shard_map/all_gather | solution.py:327
  138.0 39.5 %all-gather.17.cloned.1.call-done = bf16[1,768,768]{2,1,0:T(8,128)(2,1)} async-done(((bf16[1,48,768]{2,1,0:T(8,128)(2,1)}), bf16[1,768,768]{2,1,0:T(8,128)(2,1)}) %all-gather.17.cloned.1.call-update) | async-done | bytes 1179664 | tf_op jit(solution)/shard_map/all_gather | solution.py:328
  177.5 54.5 %all-gather.11.cloned.1.call-done = bf16[1,768,3072]{2,1,0:T(8,128)(2,1)} async-done(((bf16[1,48,3072]{2,1,0:T(8,128)(2,1)}), bf16[1,768,3072]{2,1,0:T(8,128)(2,1)}) %all-gather.11.cloned.1.call-update) | async-done | bytes 4718608 | tf_op jit(solution)/shard_map/all_gather | solution.py:329
  232.0 54.1 %all-gather.13.cloned.1.call-done = bf16[1,3072,768]{2,1,0:T(8,128)(2,1)} async-done(((bf16[1,192,768]{2,1,0:T(8,128)(2,1)}), bf16[1,3072,768]{2,1,0:T(8,128)(2,1)}) %all-gather.13.cloned.1.call-update) | async-done | bytes 4718608 | tf_op jit(solution)/shard_map/all_gather | solution.py:330
  286.2 30.5 %conditional.3 = (bf16[1,384,768]{2,1,0:T(8,128)(2,1)}, bf16[1,384,768]{2,1,0:T(8,128)(2,1)S(1)}, bf16[1,384,768]{2,1,0:T(8,128)(2,1)}, f32[1,384,768]{2,1,0:T(8...) conditional(s32[]{:T(128)} %convert_element_type.353, () %tuple.63, ...), branch_computations={%region_4.5_spmd, %region_5.8_spmd} | conditional | flops 4612128768 | bytes 54916768 | solution.py:374
  288.4 15.3 %add_bitcast_fusion = (f32[1,384,3072]{2,1,0:T(8,128)}, bf16[384,3072]{1,0:T(8,128)(2,1)}) fusion(f32[3072]{0:T(1024)S(1)} %get-tuple-element.154, bf16[768,3072]{1,0:T(8,128)(2,1)} %get-tuple-element.153, bf16[1,384,768]{2,1,0:T(8,128)(2,1)} %convert_element_type.272), kind=kOutput, calls=%fused_computation.19 | convolution fusion | flops 1889796096 | bytes 12398592 | tf_op jit(solution)/shard_map/cond/branch_1_fun/rld,de->rle/dot_general | solution.py:19
  321.8 11.2 collective-permute-done
  333.0 12.2 collective-permute-done.1
  345.2 19.5 %conditional.4 = (bf16[1,384,768]{2,1,0:T(8,128)(2,1)}, f32[1,384,768]{2,1,0:T(8,128)S(1)}, bf16[1,384,768]{2,1,0:T(8,128)(2,1)}, bf16[1,384,768]{1,2,0:T(8,128)...) conditional(s32[]{:T(128)} %convert_element_type.353, ...), branch_computations={%region_8.28_spmd, %region_28.29_spmd} | conditional | flops 10569494528 | bytes 309345216 | solution.py:400
  367.3 71.2 %collective-permute-done.2 = bf16[1,384,768]{2,1,0:T(8,128)(2,1)} collective-permute-done((bf16[1,384,768]{2,1,0:T(8,128)(2,1)}, bf16[1,384,768]{2,1,0:T(8,128)(2,1)}, u32[]{:S(2)}, u32[]{:S(2)}) %collective-permute-start.2) | collective-permute-done | bytes 589856 | tf_op jit(solution)/shard_map/ppermute | solution.py:15
  438.5 11.6 collective-permute-done.3
  450.2 45.9 %conditional.5 = (f32[1,384,768]{2,1,0:T(8,128)S(1)}, f32[4,768]{1,0:T(4,128)S(1)}, f32[1,768]{1,0:T(1,128)}, bf16[1,384,768]{2,1,0:T(8,128)(2,1)}, bf16[1,384,7...) conditional(s32[]{:T(128)} %convert_element_type.353, ...), branch_computations={%region_29.30_spmd, %region_30.40_spmd} | conditional | flops 4625402880 | bytes 99777432 | solution.py:421
  463.0 15.4 %convert_reduce_fusion.5 = (f32[3072]{0:T(1024)}, bf16[1,384,3072]{2,1,0:T(8,128)(2,1)S(1)}) fusion(f32[1,384,3072]{2,1,0:T(8,128)} %get-tuple-element.196, bf16[3072,768]{1,0:T(8,128)(2,1)S(1)} %bitcast.374, bf16[1,384,768]{2,1,0:T(8,128)(2,1)S(1)} %get-tuple-element.590), kind=kOutput, calls=%fused_computation.148 | convolution fusion | flops 1899230208 | bytes 12398592 | tf_op jit(solution)/shard_map/cond/branch_1_fun/rle,de->rld/dot_general | solution.py:23
  522.5 12.3 copy.106
  539.1 12.3 copy.107
  559.6 6.9 convolution_bitcast_fusion.4
  583.9 150.5 %all-reduce.9.cloned.1.call-done = (f32[1,768,1536]{2,0,1:T(1,128)}, f32[1,768,1536]{2,0,1:T(1,128)}) async-done(((f32[1,768,1536]{2,0,1:T(1,128)}, f32[1,768,1536]{2,0,1:T(1,128)}), (f32[1,768,1536]{2,0,1:T(1,128)}, f32[1,768,1536]{2,0,1:T(1,128)})) %all-reduce.9.cloned.1.call-update) | async-done | bytes 9437200
  737.0 127.1 %all-reduce.7.cloned.1.call-done = (f32[5,768]{1,0:T(8,128)}, f32[16,768]{1,0:T(8,128)}, f32[2,3072]{1,0:T(2,128)}) async-done(((f32[5,768]{1,0:T(8,128)}, f32[16,768]{1,0:T(8,128)}, f32[2,3072]{1,0:T(2,128)}), (f32[5,768]{1,0:T(8,128)}, f32[16,768]{1,0:T(8,128)}, f32[2,3072]{1,0:T(2,128)})) %all-reduce.7.cloned.1.call-update) | async-done | bytes 89104 | tf_op jit(solution)/shard_map/psum | solution.py:473
  864.1 68.7 %reduce-scatter.5.cloned.1.call-done = f32[1,48,768]{2,1,0:T(8,128)} async-done(((f32[1,768,768]{2,1,0:T(8,128)}), f32[1,48,768]{2,1,0:T(8,128)}) %reduce-scatter.5.cloned.1.call-update) | async-done | bytes 147472 | tf_op jit(solution)/shard_map/reduce_scatter | solution.py:436
  932.9 66.2 %reduce-scatter.7.cloned.1.call-done = f32[1,48,768]{2,1,0:T(8,128)} async-done(((f32[1,768,768]{2,1,0:T(8,128)}), f32[1,48,768]{2,1,0:T(8,128)}) %reduce-scatter.7.cloned.1.call-update) | async-done | bytes 147472 | tf_op jit(solution)/shard_map/reduce_scatter | solution.py:437
  999.0 115.7 %reduce-scatter.9.cloned.1.call-done = f32[1,48,3072]{2,1,0:T(8,128)} async-done(((f32[1,768,3072]{2,1,0:T(8,128)}), f32[1,48,3072]{2,1,0:T(8,128)}) %reduce-scatter.9.cloned.1.call-update) | async-done | bytes 589840 | tf_op jit(solution)/shard_map/reduce_scatter | solution.py:438
  1114.7 115.6 %reduce-scatter.11.cloned.1.call-done = f32[1,192,768]{2,1,0:T(8,128)} async-done(((f32[1,3072,768]{2,1,0:T(8,128)}), f32[1,192,768]{2,1,0:T(8,128)}) %reduce-scatter.11.cloned.1.call-update) | async-done | bytes 589840 | tf_op jit(solution)/shard_map/reduce_scatter | solution.py:439
  (282 shorter events, 150.3 us)
Async XLA Ops:
  7.2 48.1 %all-gather.7.cloned.1.call-start = ((), (), s32[]{:S(2)}) async-start(), calls=%async_computation.4 | async-start | bytes 2506752 | tf_op jit(solution)/shard_map/all_gather | solution.py:322
  7.9 90.6 %all-gather.9.cloned.1.call-start = ((), (), s32[]{:S(2)}) async-start(), calls=%async_computation.5 | async-start | bytes 2506752 | tf_op jit(solution)/shard_map/all_gather | solution.py:321
  8.7 129.3 %all-gather.15.cloned.1.call-start = ((), (), s32[]{:S(2)}) async-start(), calls=%async_computation.8 | async-start | bytes 1253376 | tf_op jit(solution)/shard_map/all_gather | solution.py:327
  9.4 168.1 %all-gather.17.cloned.1.call-start = ((), (), s32[]{:S(2)}) async-start(), calls=%async_computation.9 | async-start | bytes 1253376 | tf_op jit(solution)/shard_map/all_gather | solution.py:328
  10.0 222.0 %all-gather.11.cloned.1.call-start = ((), (), s32[]{:S(2)}) async-start(), calls=%async_computation.6 | async-start | bytes 5013504 | tf_op jit(solution)/shard_map/all_gather | solution.py:329
  10.6 275.6 %all-gather.13.cloned.1.call-start = ((), (), s32[]{:S(2)}) async-start(), calls=%async_computation.7 | async-start | bytes 5013504 | tf_op jit(solution)/shard_map/all_gather | solution.py:330
  11.2 723.3 %all-reduce.9.cloned.1.call-start = ((), (), s32[]{:S(2)}) async-start(), calls=%async_computation.15 | async-start | bytes 18874368
  12.7 97.4 %copy-start.54 = (f32[768]{0:T(1024)}, f32[768]{0:T(1024)S(1)}, u32[]{:S(2)}) copy-start(f32[768]{0:T(1024)S(1)} %dynamic-slice_reduce_fusion.1) | copy-start | bytes 9220
  14.4 330.8 %copy-start.59 = (f32[2,768]{1,0:T(2,128)}, f32[2,768]{1,0:T(2,128)S(1)}, u32[]{:S(2)}) copy-start(f32[2,768]{1,0:T(2,128)S(1)} %constant_dynamic-slice_fusion.1) | copy-start | bytes 18436
  15.2 271.0 %copy-start.56 = (f32[6,768]{1,0:T(8,128)}, f32[6,768]{1,0:T(8,128)S(1)}, u32[]{:S(2)}) copy-start(f32[6,768]{1,0:T(8,128)S(1)} %constant_dynamic-slice_fusion.3) | copy-start | bytes 55300
  15.4 270.7 %copy-start.70 = (f32[1,3072]{1,0:T(1,128)}, f32[1,3072]{1,0:T(1,128)S(1)}, u32[]{:S(2)}) copy-start(f32[1,3072]{1,0:T(1,128)S(1)} %constant_dynamic-slice_fusion) | copy-start | bytes 36868
  109.7 176.4 %copy-start.57 = (f32[384]{0:T(512)}, f32[384]{0:T(512)S(1)}, u32[]{:S(2)}) copy-start(f32[384]{0:T(512)S(1)} %broadcast_multiply_fusion.4) | copy-start | bytes 4612
  110.0 176.2 %copy-start.64 = (f32[384]{0:T(512)}, f32[384]{0:T(512)S(1)}, u32[]{:S(2)}) copy-start(f32[384]{0:T(512)S(1)} %multiply_reduce_fusion.8) | copy-start | bytes 4612
  110.0 176.1 %copy-start.60 = (f32[384]{0:T(512)}, f32[384]{0:T(512)S(1)}, u32[]{:S(2)}) copy-start(f32[384]{0:T(512)S(1)} %fusion.133) | copy-start | bytes 4612
  317.8 15.2 %collective-permute-start = (bf16[1,384,768]{1,2,0:T(8,128)(2,1)}, bf16[1,384,768]{1,2,0:T(8,128)(2,1)S(1)}, u32[]{:S(2)}, u32[]{:S(2)}) collective-permute-start(bf16[1,384,768]{1,2,0:T(8,128)(2,1)} %copy.96), channel_id=1, source_target_pairs={{0,16},{1,17},{2,18},{3,19},{4,20},{5,21},{6,22},{7,23},{8,24},{9,... | collective-permute-start | bytes 1769480 | tf_op jit(solution)/shard_map/ppermute | solution.py:15
  320.5 24.7 %collective-permute-start.1 = (bf16[1,384,768]{1,2,0:T(8,128)(2,1)S(1)}, bf16[1,384,768]{1,2,0:T(8,128)(2,1)S(1)}, u32[]{:S(2)}, u32[]{:S(2)}) collective-permute-start(bf16[1,384,768]{1,2,0:T(8,128)(2,1)S(1)} %copy.97), channel_id=1, source_target_pairs={{0,16},{1,17},{2,18},{3,19},{4,20},{5,21},{6,22},{7,23},{8,24},{9,... | collective-permute-start | bytes 1769480 | tf_op jit(solution)/shard_map/ppermute | solution.py:15
  364.7 73.8 %collective-permute-start.2 = (bf16[1,384,768]{2,1,0:T(8,128)(2,1)}, bf16[1,384,768]{2,1,0:T(8,128)(2,1)}, u32[]{:S(2)}, u32[]{:S(2)}) collective-permute-start(bf16[1,384,768]{2,1,0:T(8,128)(2,1)} %get-tuple-element.427), channel_id=1, source_target_pairs={{16,0},{17,1},{18,2},{19,3},{20,4},{21,5},{22,6},{23,7},{24,8},{25... | collective-permute-start | bytes 1769480 | tf_op jit(solution)/shard_map/ppermute | solution.py:15
  366.0 84.2 %collective-permute-start.3 = (bf16[1,384,768]{2,1,0:T(8,128)(2,1)S(1)}, bf16[1,384,768]{2,1,0:T(8,128)(2,1)S(1)}, u32[]{:S(2)}, u32[]{:S(2)}) collective-permute-start(bf16[1,384,768]{2,1,0:T(8,128)(2,1)S(1)} %get-tuple-element.428), channel_id=1, source_target_pairs={{16,0},{17,1},{18,2},{19,3},{20,4},{21,5},{22,6},{23,7},{24,8},{25... | collective-permute-start | bytes 1769480 | tf_op jit(solution)/shard_map/ppermute | solution.py:15
  551.5 312.6 %all-reduce.7.cloned.1.call-start = ((), (), s32[]{:S(2)}) async-start(), calls=%async_computation.14 | async-start | bytes 196608 | tf_op jit(solution)/shard_map/psum | solution.py:473
  554.8 378.1 %reduce-scatter.5.cloned.1.call-start = ((), (), s32[]{:S(2)}) async-start(), calls=%async_computation.10 | async-start | bytes 2506752 | tf_op jit(solution)/shard_map/reduce_scatter | solution.py:436
  557.1 441.9 %reduce-scatter.7.cloned.1.call-start = ((), (), s32[]{:S(2)}) async-start(), calls=%async_computation.11 | async-start | bytes 2506752 | tf_op jit(solution)/shard_map/reduce_scatter | solution.py:437
  559.5 555.2 %reduce-scatter.9.cloned.1.call-start = ((), (), s32[]{:S(2)}) async-start(), calls=%async_computation.12 | async-start | bytes 10027008 | tf_op jit(solution)/shard_map/reduce_scatter | solution.py:438
  566.5 663.8 %reduce-scatter.11.cloned.1.call-start = ((), (), s32[]{:S(2)}) async-start(), calls=%async_computation.13 | async-start | bytes 10027008 | tf_op jit(solution)/shard_map/reduce_scatter | solution.py:439
  578.5 656.0 %copy-start.1 = (f32[2,3072]{1,0:T(2,128)S(1)}, f32[2,3072]{1,0:T(2,128)}, u32[]{:S(2)}) copy-start(f32[2,3072]{1,0:T(2,128)} %param.29) | copy-start | bytes 73732
  (56 other events, 665.4 us)
Sparse Core Ops, SparseCore 0:
  10.3 44.9 all-gather.6
  57.5 40.9 all-gather.8
  100.9 37.1 all-gather.14
  140.2 37.3 all-gather.16
  179.6 52.3 all-gather.10
  234.2 51.9 all-gather.12
  551.6 182.7 all-reduce.8
  742.0 122.0 all-reduce.6
  869.0 63.8 reduce-scatter.4
  937.0 61.9 reduce-scatter.6
  1004.3 110.3 reduce-scatter.8
  1119.2 111.0 reduce-scatter.10
where the time goes:
time: 1250 us; the launch traced here: 1240 us
  waiting for transfers between devices  1010 us (81%)
  matrix products  99 us (8%)
  local copies, waits for them, and re-layouts  76.3 us (6%)
  other arithmetic  27.6 us (2%)
  between operations  15.9 us (1%)
    unnamed x13, waiting for transfers between devices  154 us
    psum x1, waiting for transfers between devices, local(): lax.psum((grad_gains, grad_biases, grad_fbias), ('section', 'dp'))  127 us
    reduce_scatter x1, waiting for transfers between devices, local(): lax.psum_scatter(grad_in[None], 'dp', scatter_dimension=1, tiled=True)  116 us
    reduce_scatter x1, waiting for transfers between devices, local(): lax.psum_scatter(grad_out[None], 'dp', scatter_dimension=1, tiled=True)  116 us
    ppermute x4, waiting for transfers between devices, from_behind(): return lax.ppermute(x, axis, pairs)  106 us
    reduce_scatter x1, waiting for transfers between devices, local(): lax.psum_scatter(grad_ca[None], 'dp', scatter_dimension=1, tiled=True)  68.7 us
    reduce_scatter x1, waiting for transfers between devices, local(): lax.psum_scatter(grad_cb[None], 'dp', scatter_dimension=1, tiled=True)  66.2 us
    all_gather x1, waiting for transfers between devices, local(): lax.all_gather(ffn_in, 'dp', axis=1, tiled=True)  54.5 us
  transfers between devices with their start and end apart: 16, of which 16 were waited for; matrix products, arithmetic and copies ran while one was open for 4% of the time, Pallas kernels for 0%

commit v1 on v0

--- a/solution.py
+++ b/solution.py
@@ -1,6 +1,8 @@
 import jax
 import jax.numpy as jnp
 from jax import lax
+from jax.experimental import pallas as pl
+from jax.experimental.pallas import tpu as pltpu
 from jax.sharding import PartitionSpec as P
 
 HEADS = 12
@@ -300,7 +302,7 @@
     return (grad_qk, grad_vo)
 
 
-def local(
+def local_any(
     tokens,
     segments,
     cotangent,
@@ -488,7 +490,595 @@
     )
 
 
+MESH = pl.DeviceIdType.MESH
+CHIPS = 8
+FAR = 3
+
+
+class Place:
+    def __init__(self):
+        self.section = lax.axis_index("section")
+        shard = lax.axis_index("dp")
+        self.core = shard % 2
+        self.chip = shard // 2
+        across = self.chip % 2
+        along = self.chip // 2
+        self.pos = along + across * (7 - 2 * along)
+
+    def chip_at(self, step):
+        spot = (self.pos + step + CHIPS) % CHIPS
+        across = spot // 4
+        along = spot + across * (7 - 2 * spot)
+        return along * 2 + across
+
+    def ring(self, step):
+        return (self.section, self.chip_at(step) * 2 + self.core)
+
+    def sibling(self):
+        return (self.section, self.chip * 2 + 1 - self.core)
+
+    def peer(self):
+        return (1 - self.section, self.chip * 2 + self.core)
+
+
+def enter(place):
+    barrier = pltpu.get_barrier_semaphore()
+    for other in (place.ring(1), place.ring(-1), place.sibling(), place.peer()):
+        pl.semaphore_signal(barrier, inc=1, device_id=other, device_id_type=MESH)
+    pl.semaphore_wait(barrier, 4)
+
+
+class Piece:
+    def __init__(self, ref, by_rows, low, span, slot):
+        self.ref, self.by_rows, self.low, self.span, self.slot = ref, by_rows, low, span, slot
+
+    def at(self, chip, core, half=None):
+        low, span = self.low, self.span
+        if half is not None:
+            span = span // 2
+            low = low + half * span
+        if self.by_rows:
+            return self.ref.at[chip, core, low : low + span, :]
+        return self.ref.at[chip, core, :, low : low + span]
+
+
+class Gather:
+    def __init__(self, place, pieces, ring_send, ring_recv, side_send, side_recv):
+        self.place, self.pieces = place, pieces
+        self.ring_send, self.ring_recv, self.side_send, self.side_recv = ring_send, ring_recv, side_send, side_recv
+
+    def ring_copy(self, p, way, hop):
+        sign = 1 - 2 * way
+        ref = self.pieces[p].at(self.place.chip_at(-sign * hop), self.place.core, way if hop == FAR else None)
+        return pltpu.make_async_remote_copy(
+            ref, ref, self.ring_send.at[p, way, hop], self.ring_recv.at[p, way, hop],
+            device_id=self.place.ring(sign), device_id_type=MESH,
+        )
+
+    def arrival(self, p, way, hop, core):
+        sign = 1 - 2 * way
+        return self.pieces[p].at(self.place.chip_at(-sign * (hop + 1)), core, way if hop == FAR else None)
+
+    def side_copy(self, p, k, core):
+        if k == 0:
+            ref = self.pieces[p].at(self.place.chip, core)
+        else:
+            ref = self.arrival(p, (k - 1) // 4, (k - 1) % 4, core)
+        return pltpu.make_async_remote_copy(
+            ref, ref, self.side_send.at[p, k], self.side_recv.at[p, k],
+            device_id=self.place.sibling(), device_id_type=MESH,
+        )
+
+    def start(self, p):
+        self.ring_copy(p, 0, 0).start()
+        self.ring_copy(p, 1, 0).start()
+        self.side_copy(p, 0, self.place.core).start()
+
+    def event(self, p, way, hop):
+        ref = self.arrival(p, way, hop, self.place.core)
+        pltpu.make_async_remote_copy(
+            ref, ref, self.ring_send.at[p, way, hop], self.ring_recv.at[p, way, hop],
+            device_id=self.place.ring(1), device_id_type=MESH,
+        ).wait_recv()
+        if hop < FAR:
+            self.ring_copy(p, way, hop + 1).start()
+        self.side_copy(p, 1 + 4 * way + hop, self.place.core).start()
+
+    def side_arrivals(self, p):
+        for k in range(9):
+            self.side_copy(p, k, 1 - self.place.core).wait_recv()
+
+    def finish(self, p):
+        for way in range(2):
+            for hop in range(4):
+                self.ring_copy(p, way, hop).wait_send()
+        for k in range(9):
+            self.side_copy(p, k, self.place.core).wait_send()
+
+
+def piece_list(qk, vo, w_in, w_out, cross):
+    return [
+        Piece(qk, False, 0, 1536, 0),
+        Piece(vo, False, 0, 1536, 1),
+        Piece(w_in, False, 0, 1536, 2),
+        Piece(w_in, False, 1536, 1536, 3),
+        Piece(w_out, True, 0, 96, 0),
+        Piece(w_out, True, 96, 96, 1),
+        Piece(cross, False, 0, 1536, 4),
+        Piece(cross, False, 1536, 1536, 5),
+    ]
+
+
+def gather_kernel(qk, vo, cqk, cvo, fin, fout, w_qk, w_vo, w_in, w_out, w_x, local_sem, x_send, x_recv, rs, rr, ss, sr):
+    place = Place()
+    chip, core = place.chip, place.core
+    width = cqk.shape[-1]
+    copies = [
+        pltpu.make_async_copy(src.at[0], dst.at[chip, core], local_sem.at[i])
+        for i, (src, dst) in enumerate([(qk, w_qk), (vo, w_vo), (fin, w_in), (fout, w_out)])
+    ]
+    for copy in copies:
+        copy.start()
+    enter(place)
+    decoder = place.section == 1
+    own_cross = [
+        pltpu.make_async_copy(src.at[0], w_x.at[chip, core, :, i * width : (i + 1) * width], local_sem.at[4 + i])
+        for i, src in enumerate([cqk, cvo])
+    ]
+    from_encoder = [
+        pltpu.make_async_remote_copy(
+            src.at[0], w_x.at[chip, core, :, (2 + i) * width : (3 + i) * width], x_send.at[i], x_recv.at[i],
+            device_id=place.peer(), device_id_type=MESH,
+        )
+        for i, src in enumerate([cqk, cvo])
+    ]
+
+    @pl.when(place.section == 0)
+    def _():
+        for copy in from_encoder:
+            copy.start()
+
+    @pl.when(decoder)
+    def _():
+        for copy in own_cross:
+            copy.start()
+
+    for copy in copies:
+        copy.wait()
+    gather = Gather(place, piece_list(w_qk, w_vo, w_in, w_out, w_x), rs, rr, ss, sr)
+    gather.start(0)
+    gather.start(1)
+    for pair in range(3):
+        for hop in range(4):
+            for p in (2 * pair, 2 * pair + 1):
+                for way in range(2):
+                    gather.event(p, way, hop)
+                if hop == 2 and p + 2 < 6:
+                    gather.start(p + 2)
+
+    @pl.when(decoder)
+    def _():
+        for copy in own_cross:
+            copy.wait()
+        for copy in from_encoder:
+            copy.wait_recv()
+        gather.start(6)
+        gather.start(7)
+        for hop in range(4):
+            for p in (6, 7):
+                for way in range(2):
+                    gather.event(p, way, hop)
+        for p in (6, 7):
+            gather.side_arrivals(p)
+            gather.finish(p)
+
+    @pl.when(place.section == 0)
+    def _():
+        for copy in from_encoder:
+            copy.wait_send()
+
+    for p in range(6):
+        gather.side_arrivals(p)
+        gather.finish(p)
+
+
+def gather_weights(qk, vo, cqk, cvo, fin, fout):
+    def whole(shard, columns):
+        return jax.ShapeDtypeStruct((CHIPS, 2, shard.shape[1], columns), shard.dtype)
+
+    any_space = pl.BlockSpec(memory_space=pl.ANY)
+    return pl.pallas_call(
+        gather_kernel,
+        out_shape=(
+            whole(qk, qk.shape[2]), whole(vo, vo.shape[2]), whole(fin, fin.shape[2]), whole(fout, fout.shape[2]),
+            whole(cqk, 4 * cqk.shape[2]),
+        ),
+        in_specs=[any_space] * 6,
+        out_specs=(any_space,) * 5,
+        scratch_shapes=[
+            pltpu.SemaphoreType.DMA((6,)),
+            pltpu.SemaphoreType.DMA((2,)),
+            pltpu.SemaphoreType.DMA((2,)),
+            pltpu.SemaphoreType.DMA((8, 2, 4)),
+            pltpu.SemaphoreType.DMA((8, 2, 4)),
+            pltpu.SemaphoreType.DMA((8, 9)),
+            pltpu.SemaphoreType.DMA((8, 9)),
+        ],
+        compiler_params=pltpu.CompilerParams(collective_id=0, has_side_effects=True),
+        name="gather_weights",
+    )(qk, vo, cqk, cvo, fin, fout)
+
+
+class Scatter:
+    def __init__(self, place, pieces, side_c, side_r, land_c, land_r, ring_send, ring_recv, side_send, side_recv):
+        self.place, self.pieces = place, pieces
+        self.side_c, self.side_r, self.land_c, self.land_r = side_c, side_r, land_c, land_r
+        self.ring_send, self.ring_recv, self.side_send, self.side_recv = ring_send, ring_recv, side_send, side_recv
+
+    def cut(self, p, ref, half):
+        piece = self.pieces[p]
+        if half is None:
+            return ref
+        span = piece.span // 2
+        if piece.by_rows:
+            return ref.at[half * span : (half + 1) * span, :]
+        return ref.at[:, half * span : (half + 1) * span]
+
+    def from_side(self, p, chip, half=None):
+        piece = self.pieces[p]
+        return self.cut(p, (self.side_r if piece.by_rows else self.side_c).at[piece.slot, chip], half)
+
+    def landed(self, p, way, step, half=None):
+        piece = self.pieces[p]
+        return self.cut(p, (self.land_r if piece.by_rows else self.land_c).at[piece.slot, way, step], half)
+
+    def side_copy(self, p):
+        piece = self.pieces[p]
+        span = slice(piece.low, piece.low + piece.span)
+        other = 1 - self.place.core
+        src = piece.ref.at[:, other, span, :] if piece.by_rows else piece.ref.at[:, other, :, span]
+        dst = (self.side_r if piece.by_rows else self.side_c).at[piece.slot]
+        return pltpu.make_async_remote_copy(
+            src, dst, self.side_send.at[p], self.side_recv.at[p],
+            device_id=self.place.sibling(), device_id_type=MESH,
+        )
+
+    def chip_of(self, way, step):
+        sign = 1 - 2 * way
+        return self.place.chip_at(sign * (4 - step))
+
+    def ring_copy(self, p, way, step):
+        sign = 1 - 2 * way
+        half = way if step == 0 else None
+        return pltpu.make_async_remote_copy(
+            self.pieces[p].at(self.chip_of(way, step), self.place.core, half), self.landed(p, way, step, half),
+            self.ring_send.at[p, way, step], self.ring_recv.at[p, way, step],
+            device_id=self.place.ring(sign), device_id_type=MESH,
+        )
+
+    def start(self, p):
+        self.side_copy(p).wait_recv()
+        for way in range(2):
+            chip = self.chip_of(way, 0)
+            own = self.pieces[p].at(chip, self.place.core, way)
+            total = own[...].astype(jnp.float32) + self.from_side(p, chip, way)[...].astype(jnp.float32)
+            own[...] = total.astype(jnp.bfloat16)
+            self.ring_copy(p, way, 0).start()
+
+    def event(self, p, way, step):
+        self.ring_copy(p, way, step).wait_recv()
+        chip = self.chip_of(way, step + 1)
+        for half in range(2):
+            own = self.pieces[p].at(chip, self.place.core, half)
+            total = own[...].astype(jnp.float32) + self.from_side(p, chip, half)[...].astype(jnp.float32)
+            if step > 0 or half == way:
+                total = total + self.landed(p, way, step, half)[...].astype(jnp.float32)
+            own[...] = total.astype(jnp.bfloat16)
+        self.ring_copy(p, way, step + 1).start()
+
+    def last(self, p):
+        chip = self.place.chip
+        total = self.pieces[p].at(chip, self.place.core)[...].astype(jnp.float32)
+        total = total + self.from_side(p, chip)[...].astype(jnp.float32)
+        for way in range(2):
+            self.ring_copy(p, way, 3).wait_recv()
+            total = total + self.landed(p, way, 3)[...].astype(jnp.float32)
+        return total
+
+    def finish(self, p):
+        self.side_copy(p).wait_send()
+        for way in range(2):
+            for step in range(4):
+                self.ring_copy(p, way, step).wait_send()
+
+
+def scatter_kernel(
+    i_qk, i_vo, i_in, i_out, i_x, o_qk, o_vo, o_cqk, o_cvo, o_in, o_out,
+    g_qk, g_vo, g_in, g_out, g_x, side_c, side_r, land_c, land_r, x_total, x_land,
+    local_sem, x_send, x_recv, rs, rr, ss, sr,
+):
+    place = Place()
+    decoder = place.section == 1
+    copies = [
+        pltpu.make_async_copy(src, dst, local_sem.at[i])
+        for i, (src, dst) in enumerate([(i_qk, g_qk), (i_vo, g_vo), (i_in, g_in), (i_out, g_out), (i_x, g_x)])
+    ]
+    for copy in copies:
+        copy.start()
+    enter(place)
+    scatter = Scatter(
+        place, piece_list(g_qk, g_vo, g_in, g_out, g_x), side_c, side_r, land_c, land_r, rs, rr, ss, sr
+    )
+    for copy in copies:
+        copy.wait()
+    for p in range(6):
+        scatter.side_copy(p).start()
+    to_encoder = pltpu.make_async_remote_copy(
+        x_total, x_land, x_send.at[0], x_recv.at[0], device_id=place.peer(), device_id_type=MESH
+    )
+    width = o_cqk.shape[-1]
+
+    @pl.when(decoder)
+    def _():
+        for p in (6, 7):
+            scatter.side_copy(p).start()
+        for p in (6, 7):
+            scatter.start(p)
+        for step in range(3):
+            for p in (6, 7):
+                for way in range(2):
+                    scatter.event(p, way, step)
+        total = scatter.last(6)
+        o_cqk[0] = total[:, :width]
+        o_cvo[0] = total[:, width:]
+        x_total[...] = scatter.last(7)
+        to_encoder.start()
+
+    scatter.start(0)
+    scatter.start(1)
+    for pair in range(3):
+        for step in range(3):
+            for p in (2 * pair, 2 * pair + 1):
+                for way in range(2):
+                    scatter.event(p, way, step)
+                if step == 2 and p + 2 < 6:
+                    scatter.start(p + 2)
+        if pair == 0:
+            o_qk[0] = scatter.last(0)
+            o_vo[0] = scatter.last(1)
+        elif pair == 1:
+            o_in[0, :, :1536] = scatter.last(2)
+            o_in[0, :, 1536:] = scatter.last(3)
+        else:
+            o_out[0, :96] = scatter.last(4)
+            o_out[0, 96:] = scatter.last(5)
+
+    @pl.when(decoder)
+    def _():
+        to_encoder.wait_send()
+        for p in (6, 7):
+            scatter.finish(p)
+
+    @pl.when(place.section == 0)
+    def _():
+        to_encoder.wait_recv()
+        o_cqk[0] = x_land[:, :width]
+        o_cvo[0] = x_land[:, width:]
+
+    for p in range(6):
+        scatter.finish(p)
+
+
+def scatter_grads(g_qk, g_vo, g_in, g_out, g_x):
+    def mine(shape):
+        return jax.ShapeDtypeStruct(shape, jnp.float32)
+
+    any_space = pl.BlockSpec(memory_space=pl.ANY)
+    in_vmem = pl.BlockSpec(memory_space=pltpu.VMEM)
+    return pl.pallas_call(
+        scatter_kernel,
+        out_shape=(
+            mine((1, 48, 1536)), mine((1, 48, 1536)), mine((1, 48, 768)), mine((1, 48, 768)),
+            mine((1, 48, 3072)), mine((1, 192, 768)),
+        ),
+        in_specs=[any_space] * 5,
+        out_specs=(in_vmem,) * 6,
+        scratch_shapes=[pltpu.VMEM(g.shape, jnp.bfloat16) for g in (g_qk, g_vo, g_in, g_out, g_x)]
+        + [
+            pltpu.VMEM((6, CHIPS, 48, 1536), jnp.bfloat16),
+            pltpu.VMEM((2, CHIPS, 96, 768), jnp.bfloat16),
+            pltpu.VMEM((6, 2, 4, 48, 1536), jnp.bfloat16),
+            pltpu.VMEM((2, 2, 4, 96, 768), jnp.bfloat16),
+            pltpu.VMEM((48, 1536), jnp.float32),
+            pltpu.VMEM((48, 1536), jnp.float32),
+            pltpu.SemaphoreType.DMA((5,)),
+            pltpu.SemaphoreType.DMA((1,)),
+            pltpu.SemaphoreType.DMA((1,)),
+            pltpu.SemaphoreType.DMA((8, 2, 4)),
+            pltpu.SemaphoreType.DMA((8, 2, 4)),
+            pltpu.SemaphoreType.DMA((8,)),
+            pltpu.SemaphoreType.DMA((8,)),
+        ],
+        compiler_params=pltpu.CompilerParams(
+            collective_id=1, has_side_effects=True, vmem_limit_bytes=56 * 1024 * 1024
+        ),
+        name="scatter_grads",
+    )(g_qk, g_vo, g_in, g_out, g_x)
+
+
+def local_ring(
+    tokens,
+    segments,
+    cotangent,
+    attn_qk,
+    attn_vo,
+    cross_qk,
+    cross_vo,
+    ffn_in,
+    ffn_out,
+    gains,
+    biases,
+    ffn_bias,
+):
+    head_count = HEADS
+    section_index = lax.axis_index("section")
+    is_enc = section_index == 0
+    model_width = tokens.shape[-1]
+    w_qk, w_vo, w_in, w_out, w_x = (
+        whole.reshape(-1, whole.shape[-1])
+        for whole in gather_weights(attn_qk, attn_vo, cross_qk, cross_vo, ffn_in, ffn_out)
+    )
+    w_cq, w_co, w_ck, w_cv = (w_x[:, i * model_width : (i + 1) * model_width] for i in range(4))
+    section_bias = lax.dynamic_slice_in_dim(biases, 6 * section_index, 6, 0)
+    section_gain = lax.dynamic_slice_in_dim(gains, 2 * section_index, 2, 0)
+    bias_in = lax.dynamic_index_in_dim(ffn_bias, section_index, 0, keepdims=False)
+    section_seg = lax.dynamic_index_in_dim(segments, section_index, 0, keepdims=False)
+    length = tokens.shape[2]
+    position = jnp.arange(length)
+    earlier = position[None, :] <= position[:, None]
+    allowed_self = (section_seg[:, :, None] == section_seg[:, None, :]) & (earlier[None] | is_enc)
+    allowed_cross = segments[1][:, :, None] == segments[0][:, None, :]
+    source = tokens[0]
+    hidden_one, kept_self = self_forward(
+        source, w_qk, w_vo, section_bias, section_gain[0], allowed_self, head_count
+    )
+
+    def run_encoder():
+        branch, kept = ffn_forward(hidden_one, w_in, w_out, bias_in, section_bias[4])
+        resid = hidden_one + branch
+        return norm_rows(resid, section_gain[1], section_bias[5]).astype(jnp.bfloat16), resid, kept
+
+    def skip_encoder():
+        flat = jnp.zeros(hidden_one.shape, jnp.bfloat16)
+        wide_shape = (hidden_one.shape[0], hidden_one.shape[1], w_in.shape[1])
+        return (
+            flat,
+            jnp.zeros_like(hidden_one),
+            (flat, jnp.zeros(wide_shape, jnp.float32), jnp.zeros(wide_shape, jnp.bfloat16)),
+        )
+
+    memory, enc_resid, enc_kept = lax.cond(is_enc, run_encoder, skip_encoder)
+    got_memory = from_behind(memory, "section", 1)
+
+    def run_decoder():
+        key_rows = product(got_memory, w_ck).astype(jnp.bfloat16)
+        value_rows = (product(got_memory, w_cv) + biases[13]).astype(jnp.bfloat16)
+        decoded, grad_keys, grad_values, tail = decoder_step(
+            hidden_one,
+            w_cq,
+            w_co,
+            w_in,
+            w_out,
+            bias_in,
+            section_bias,
+            section_gain[1],
+            gains[4],
+            biases[12:16],
+            key_rows,
+            value_rows,
+            allowed_cross,
+            cotangent,
+            head_count,
+        )
+        grad_memory = back_product(grad_keys, w_ck) + back_product(grad_values, w_cv)
+        grad_hidden, operands, grad_bin, grad_bout, grad_gain, grad_shift, cross_rows, grad_gain_cross = tail
+        cross_rows = cross_rows.at[1].set(column_sum(grad_values))
+        grad_x = jnp.concatenate(
+            [
+                weight_grad(operands[0], operands[1]),
+                weight_grad(operands[2], operands[3]),
+                weight_grad(got_memory, grad_keys),
+                weight_grad(got_memory, grad_values),
+            ],
+            axis=1,
+        ).astype(jnp.bfloat16)
+        return (
+            decoded,
+            grad_memory.astype(jnp.bfloat16),
+            grad_x,
+            (grad_hidden, operands[4:], grad_bin, grad_bout, grad_gain, grad_shift, cross_rows, grad_gain_cross),
+        )
+
+    def skip_decoder():
+        flat = jnp.zeros(hidden_one.shape, jnp.bfloat16)
+        tail = zero_tail(hidden_one, w_in)
+        return (flat, flat, jnp.zeros(w_x.shape, jnp.bfloat16), (tail[0], tail[1][4:]) + tail[2:])
+
+    decoded, grad_memory, grad_x, dec_tail = lax.cond(is_enc, skip_decoder, run_decoder)
+    back_memory = from_behind(grad_memory, "section", -1).astype(jnp.float32)
+
+    def run_encoder_back():
+        grad_last, grad_gain, grad_shift = norm_back(enc_resid, section_gain[1], section_bias[5], back_memory)
+        grad_ffn, ffn_ops, grad_bin, grad_bout = ffn_backward(w_in, w_out, enc_kept, grad_last)
+        zero_line = jnp.zeros_like(grad_gain)
+        return (
+            grad_last + grad_ffn,
+            ffn_ops,
+            grad_bin,
+            grad_bout,
+            grad_gain,
+            grad_shift,
+            jnp.zeros((4, model_width), jnp.float32),
+            zero_line,
+        )
+
+    def keep_decoder():
+        return dec_tail
+
+    tail_result = lax.cond(is_enc, run_encoder_back, keep_decoder)
+    (
+        grad_hidden,
+        tail_ops,
+        grad_bin,
+        grad_bout,
+        grad_gain_last,
+        grad_shift_last,
+        cross_rows,
+        grad_gain_cross,
+    ) = tail_result
+    layer_out = jnp.where(is_enc, memory, decoded)
+    grad_in = weight_grad(tail_ops[0], tail_ops[1]).astype(jnp.bfloat16)
+    grad_out = weight_grad(tail_ops[2], tail_ops[3]).astype(jnp.bfloat16)
+    grad_source, self_ops, self_rows, grad_gain_first = self_backward(
+        source,
+        w_qk,
+        w_vo,
+        section_bias,
+        section_gain[0],
+        allowed_self,
+        head_count,
+        kept_self,
+        grad_hidden,
+    )
+    grad_qk, grad_vo = self_whole(self_ops)
+
+    def blocks(grad):
+        return grad.astype(jnp.bfloat16).reshape(CHIPS, 2, -1, grad.shape[-1])
+
+    large_parts = scatter_grads(blocks(grad_qk), blocks(grad_vo), blocks(grad_in), blocks(grad_out), blocks(grad_x))
+    section_rows = jnp.concatenate([self_rows, jnp.stack([grad_bout, grad_shift_last])], axis=0)
+    bias_block = lax.dynamic_update_slice_in_dim(
+        jnp.zeros((12, model_width), jnp.float32), section_rows, 6 * section_index, 0
+    )
+    grad_biases = jnp.concatenate([bias_block, cross_rows], axis=0)
+    gain_block = lax.dynamic_update_slice_in_dim(
+        jnp.zeros((4, model_width), jnp.float32),
+        jnp.stack([grad_gain_first, grad_gain_last]),
+        2 * section_index,
+        0,
+    )
+    grad_gains = jnp.concatenate([gain_block, grad_gain_cross[None]], axis=0)
+    grad_fbias = lax.dynamic_update_slice_in_dim(
+        jnp.zeros_like(ffn_bias), grad_bin[None], section_index, 0
+    )
+    sum_gains, sum_biases, sum_fbias = lax.psum(
+        (grad_gains, grad_biases, grad_fbias), ("section", "dp")
+    )
+    return (layer_out[None], grad_source[None]) + tuple(large_parts) + (sum_gains, sum_biases, sum_fbias)
+
+
 def solution(mesh):
+    any_size = mesh.shape["section"] != 2 or mesh.shape["dp"] != 2 * CHIPS
     placed = (
         P("section", "dp", None, None),
         P(None, "dp", None),
@@ -504,7 +1094,7 @@
         P(),
     )
     return jax.shard_map(
-        local,
+        local_any if any_size else local_ring,
         mesh=mesh,
         in_specs=placed,
         out_specs=(

time: 1250 us -> 521 us (0.42)
  waiting for transfers between devices: 1010 us -> 146 us
  Pallas kernels: 0 us -> 186 us
  local copies, waits for them, and re-layouts: 76.3 us -> 43.3 us
  matrix products: 99 us -> 81.5 us
    reduce_scatter x4 -> x0, waiting for transfers between devices: 366 us -> none  [the longest x1 116 us: local(): lax.psum_scatter(grad_in[None], 'dp', scatter_dimension=1, tiled=True)]
    all_gather x6 -> x0, waiting for transfers between devices: 256 us -> none  [the longest x1 54.5 us: local(): lax.all_gather(ffn_in, 'dp', axis=1, tiled=True)]
    pallas_call x0 -> x2, Pallas kernels: none -> 186 us  [the longest x1 104 us: gather_weights(): pl.pallas_call(gather_kernel, out_shape=(whole(qk, qk.shape[2]), whole(vo...]
    unnamed x13 -> x1, waiting for transfers between devices: 154 us -> 0.02 us
    psum x1, waiting for transfers between devices: 127 us -> 35.4 us  [local_ring(): lax.psum((grad_gains, grad_biases, grad_fbias), ('section', 'dp'))]
    broadcast_in_dim x4 -> x3, local copies, waits for them, and re-layouts: 24.6 us -> 0.01 us  [the longest x1 0.01 us: local_ring(): jnp.zeros_like(ffn_bias)]
    dot_general x8 -> x6, matrix products: 31.2 us -> 26.2 us  [product(): jnp.einsum('rld,de->rle', left, right, preferred_element_type=jnp.float32)]
    dot_general x7 -> x5, matrix products: 29.6 us -> 25 us  [back_product(): jnp.einsum('rle,de->rld', grad, right, preferred_element_type=jnp.float32)]
  transfers between devices with their start and end apart: 16 -> 3, of which waited for: 16 -> 3; matrix products, arithmetic and copies ran while one was open for 4% -> 1% of each run, Pallas kernels for 0% -> 16%
where the time goes in v1:
time: 521 us; the launch traced here: 518 us
  Pallas kernels  186 us (36%)
  waiting for transfers between devices  146 us (28%)
  matrix products  81.5 us (16%)
  local copies, waits for them, and re-layouts  43.3 us (8%)
  other arithmetic  26.8 us (5%)
  between operations  15.1 us (3%)
  starting transfers between devices  12.7 us (2%)
  loops' own time  6.68 us (1%)
    ppermute x2, waiting for transfers between devices, from_behind(): return lax.ppermute(x, axis, pairs)  110 us
    pallas_call x1, Pallas kernels, gather_weights(): pl.pallas_call(gather_kernel, out_shape=(whole(qk, qk.shape[2]), whole(vo...  104 us
    pallas_call x1, Pallas kernels, scatter_grads(): pl.pallas_call(scatter_kernel, out_shape=(mine((1, 48, 1536)), mine((1, 4...  82.5 us
    psum x1, waiting for transfers between devices, local_ring(): lax.psum((grad_gains, grad_biases, grad_fbias), ('section', 'dp'))  35.4 us
    dot_general x6, matrix products, product(): jnp.einsum('rld,de->rle', left, right, preferred_element_type=jnp.float32)  26.2 us
    dot_general x5, matrix products, back_product(): jnp.einsum('rle,de->rld', grad, right, preferred_element_type=jnp.float32)  25 us
    unnamed x109, local copies, waits for them, and re-layouts  20.1 us
    dot_general x5, matrix products, weight_grad(): jnp.einsum('rld,rle->de', left, grad, preferred_element_type=jnp.float32)  15.6 us
  transfers between devices with their start and end apart: 3, of which 3 were waited for; matrix products, arithmetic and copies ran while one was open for 1% of the time, Pallas kernels for 16%

profile of v1, /device:TPU:0, one launch (start us, length us, event | category | flops | bytes accessed | tf_op | source)
XLA Modules:
  0.0 518.2 jit_solution(1969631984056184023)
XLA Ops:
  8.1 103.9 %gather_weights.1 = (bf16[8,2,48,1536]{3,2,1,0:T(8,128)(2,1)}, bf16[8,2,48,1536]{3,2,1,0:T(8,128)(2,1)}, bf16[8,2,48,3072]{3,2,1,0:T(8,128)(2,1)}, bf16[8,2,192,...) custom-call(bf16[1,48,1536]{2,1,0:T(8,128)(2,1)} %qk.1, bf16[1,48,1536]{2,1,0:T(8,128)(2,1)} %vo.1, bf16[1,48,768]{2,1,0:T(8,128)(2,1)} %cqk.1, ...), custom_call_target="tpu_custom_call" | custom-call | tf_op jit(solution)/shard_map/gather_weights/pallas_call | solution.py:690
  116.1 2.2 fusion.114
  129.5 22.3 %conditional.3 = (bf16[1,384,768]{2,1,0:T(8,128)(2,1)S(1)}, f32[1,384,768]{2,1,0:T(8,128)}, bf16[1,384,768]{2,1,0:T(8,128)(2,1)}, f32[1,384,3072]{2,1,0:T(8,128)S(1)}, bf16[1,384,3072]{2,1,0:T(8,128)(2,1)}) conditional(s32[]{:T(128)} %convert_element_type.389, () %tuple.66, (f32[1,384,768]{2,1,0:T(8,128)S(1)}, bf16[768,3072]{1,0:T(8,128)(2,1)S(1)}, ...), branch_computations={%region_4.5_spmd, %region_5.8_spmd} | conditional | flops 3705274624 | bytes 28955204 | solution.py:960
  129.9 14.1 %add_bitcast_fusion = (f32[1,384,3072]{2,1,0:T(8,128)S(1)}, bf16[384,3072]{1,0:T(8,128)(2,1)}) fusion(f32[3072]{0:T(1024)S(1)} %get-tuple-element.163, bf16[768,3072]{1,0:T(8,128)(2,1)S(1)} %get-tuple-element.162, bf16[1,384,768]{2,1,0:T(8,128)(2,1)S(1)} %convert_element_type.304), kind=kOutput, calls=%fused_computation.19 | convolution fusion | flops 1889796096 | bytes 12398592 | tf_op jit(solution)/shard_map/cond/branch_1_fun/rld,de->rle/dot_general | solution.py:21
  144.0 4.7 fusion.147
  151.8 11.3 %collective-permute-start = (bf16[1,384,768]{2,1,0:T(8,128)(2,1)S(1)}, bf16[1,384,768]{2,1,0:T(8,128)(2,1)S(1)}, u32[]{:S(2)}, u32[]{:S(2)}) collective-permute-start(bf16[1,384,768]{2,1,0:T(8,128)(2,1)S(1)} %get-tuple-element.254), channel_id=1, source_target_pairs={{0,16},{1,17},{2,18},{3,19},{4,20},{5,21},{6,22},{7,23},{8,24},{9,... | collective-permute-start | bytes 1769480 | tf_op jit(solution)/shard_map/ppermute | solution.py:17
  163.2 13.1 %collective-permute-done = bf16[1,384,768]{2,1,0:T(8,128)(2,1)S(1)} collective-permute-done((bf16[1,384,768]{2,1,0:T(8,128)(2,1)S(1)}, bf16[1,384,768]{2,1,0:T(8,128)(2,1)S(1)}, u32[]{:S(2)}, u32[]{:S(2)}) %collective-permute-start) | collective-permute-done | bytes 589856 | tf_op jit(solution)/shard_map/ppermute | solution.py:17
  176.3 19.9 %conditional.4 = (bf16[1,384,768]{2,1,0:T(8,128)(2,1)}, bf16[1,384,768]{2,1,0:T(8,128)(2,1)}, f32[1,384,768]{2,1,0:T(8,128)}, bf16[1,384,768]{2,1,0:T(8,128)(2,1...) conditional(s32[]{:T(128)} %convert_element_type.389, ...), branch_computations={%region_8.29_spmd, %region_29.30_spmd} | conditional | flops 14216965120 | bytes 357687936 | solution.py:1007
  193.4 2.8 reshape.1134
  199.4 97.3 %collective-permute-done.1 = bf16[1,384,768]{2,1,0:T(8,128)(2,1)S(1)} collective-permute-done((bf16[1,384,768]{2,1,0:T(8,128)(2,1)}, bf16[1,384,768]{2,1,0:T(8,128)(2,1)S(1)}, u32[]{:S(2)}, u32[]{:S(2)}) %collective-permute-start.1) | collective-permute-done | bytes 589856 | tf_op jit(solution)/shard_map/ppermute | solution.py:17
  296.9 31.1 %conditional.5 = (f32[1,384,768]{2,1,0:T(8,128)}, f32[4,768]{1,0:T(4,128)S(1)}, f32[1,768]{1,0:T(1,128)S(1)}, bf16[1,384,768]{2,1,0:T(8,128)(2,1)}, bf16[1,384,3...) conditional(s32[]{:T(128)} %convert_element_type.389, ...), branch_computations={%region_30.31_spmd, %region_31.40_spmd} | conditional | flops 3718542848 | bytes 85016320 | solution.py:1028
  300.9 2.4 multiply_reduce_fusion.6
  306.0 14.7 %convert_reduce_fusion.6 = (f32[3072]{0:T(1024)}, bf16[1,384,3072]{2,1,0:T(8,128)(2,1)S(1)}) fusion(f32[1,384,3072]{2,1,0:T(8,128)S(1)} %copy-done.16, bf16[3072,768]{1,0:T(8,128)(2,1)} %get-tuple-element.194, bf16[1,384,768]{2,1,0:T(8,128)(2,1)S(1)} %get-tuple-element.432), kind=kOutput, calls=%fused_computation.170 | convolution fusion | flops 1899230208 | bytes 12398592 | tf_op jit(solution)/shard_map/cond/branch_1_fun/rle,de->rld/dot_general | solution.py:25
  320.7 3.1 fusion.94
  324.6 3.2 copy.120
  335.9 4.6 convert_reduce_fusion.9
  340.6 4.4 multiply_reduce_fusion.9
  345.0 4.8 multiply_convert_fusion.2
  358.8 5.6 %convolution_convert_fusion.7 = bf16[768,3072]{1,0:T(8,128)(2,1)} fusion(bf16[1,384,3072]{2,1,0:T(8,128)(2,1)S(1)} %copy-done.71, bf16[1,384,768]{2,1,0:T(8,128)(2,1)} %get-tuple-element.274), kind=kOutput, calls=%fused_computation.212 | convolution fusion | flops 1814298624 | bytes 7667712 | tf_op jit(solution)/shard_map/rld,rle->de/dot_general | solution.py:29
  364.4 4.4 convolution_convert_fusion.6
  370.5 4.1 fusion.110
  374.7 4.1 convolution_convert_fusion.8
  378.7 82.5 %scatter_grads.1 = (f32[1,48,1536]{2,1,0:T(8,128)}, f32[1,48,1536]{2,1,0:T(8,128)}, f32[1,48,768]{2,1,0:T(8,128)}, f32[1,48,768]{2,1,0:T(8,128)}, f32[1,48,3072]{2,1,0:T(8,128)}, /*index=5*/f32[1,192,768]{2,1,0:T(8,128)}) custom-call(bf16[8,2,48,1536]{3,2,1,0:T(8,128)(2,1)} %bitcast.334, bf16[8,2,48,1536]{3,2,1,0:T(8,128)(2,1)} %pad_maximum_fusion.2.i_vo, ...), custom_call_target="tpu_custom_call" | custom-call | tf_op jit(solution)/shard_map/scatter_grads/pallas_call | solution.py:878
  461.2 35.4 %all-reduce.3.cloned.1.call-done = (f32[5,768]{1,0:T(8,128)}, f32[16,768]{1,0:T(8,128)}, f32[2,3072]{1,0:T(2,128)}) async-done(((f32[5,768]{1,0:T(8,128)}, f32[16,768]{1,0:T(8,128)}, f32[2,3072]{1,0:T(2,128)}), (f32[5,768]{1,0:T(8,128)}, f32[16,768]{1,0:T(8,128)}, f32[2,3072]{1,0:T(2,128)})) %all-reduce.3.cloned.1.call-update) | async-done | bytes 89104 | tf_op jit(solution)/shard_map/psum | solution.py:1074
  (210 shorter events, 73.7 us)
Async XLA Ops:
  7.2 120.3 %copy-start = (f32[2,3072]{1,0:T(2,128)S(1)}, f32[2,3072]{1,0:T(2,128)}, u32[]{:S(2)}) copy-start(f32[2,3072]{1,0:T(2,128)} %param.31) | copy-start | bytes 73732
  7.2 111.3 %copy-start.40 = (bf16[1,1,384,768]{3,2,1,0:T(8,128)(2,1)S(1)}, bf16[1,1,384,768]{3,2,1,0:T(8,128)(2,1)}, u32[]{:S(2)}) copy-start(bf16[1,1,384,768]{3,2,1,0:T(8,128)(2,1)} %param.20) | copy-start | bytes 1769476
  7.2 111.1 %copy-start.64 = (s32[2,1,384]{2,1,0:T(1,128)S(1)}, s32[2,1,384]{2,1,0:T(1,128)}, u32[]{:S(2)}) copy-start(s32[2,1,384]{2,1,0:T(1,128)} %param.21) | copy-start | bytes 9220
  7.2 489.4 %all-reduce.3.cloned.1.call-start = ((), (), s32[]{:S(2)}) async-start(), calls=%async_computation | async-start | bytes 196608 | tf_op jit(solution)/shard_map/psum | solution.py:1074
  114.3 7.7 %copy-start.19 = (bf16[768,384]{1,0:T(8,128)(2,1)}, bf16[768,384]{1,0:T(8,128)(2,1)S(1)}, u32[]{:S(2)}) copy-start(bf16[768,384]{1,0:T(8,128)(2,1)S(1)} %convolution_convert_fusion.12) | copy-start | bytes 1769476
  115.1 61.2 %copy-start.52 = (f32[2,768]{1,0:T(2,128)}, f32[2,768]{1,0:T(2,128)S(1)}, u32[]{:S(2)}) copy-start(f32[2,768]{1,0:T(2,128)S(1)} %constant_dynamic-slice_fusion.1) | copy-start | bytes 18436
  116.0 11.5 %copy-start.48 = (f32[768]{0:T(1024)}, f32[768]{0:T(1024)S(1)}, u32[]{:S(2)}) copy-start(f32[768]{0:T(1024)S(1)} %get-tuple-element.376) | copy-start | bytes 9220
  129.5 46.8 %copy-start.65 = (s32[2,1,384]{2,1,0:T(1,128)S(1)}, s32[2,1,384]{2,1,0:T(1,128)}, u32[]{:S(2)}) copy-start(s32[2,1,384]{2,1,0:T(1,128)} %param.21) | copy-start | bytes 9220
  129.9 14.1 %copy-start.26 = (bf16[1,384,768]{2,1,0:T(8,128)(2,1)}, bf16[1,384,768]{2,1,0:T(8,128)(2,1)S(1)}, u32[]{:S(2)}) copy-start(bf16[1,384,768]{2,1,0:T(8,128)(2,1)S(1)} %convert_element_type.304) | copy-start | bytes 1769476 | tf_op jit(solution)/shard_map/cond
  151.8 24.4 %copy-start.15 = (f32[1,384,3072]{2,1,0:T(8,128)}, f32[1,384,3072]{2,1,0:T(8,128)S(1)}, u32[]{:S(2)}) copy-start(f32[1,384,3072]{2,1,0:T(8,128)S(1)} %get-tuple-element.270) | copy-start | bytes 14155780
  151.8 24.4 %copy-start.28 = (bf16[1,384,768]{2,1,0:T(8,128)(2,1)}, bf16[1,384,768]{2,1,0:T(8,128)(2,1)S(1)}, u32[]{:S(2)}) copy-start(bf16[1,384,768]{2,1,0:T(8,128)(2,1)S(1)} %get-tuple-element.254) | copy-start | bytes 1769476
  151.8 24.4 %collective-permute-start = (bf16[1,384,768]{2,1,0:T(8,128)(2,1)S(1)}, bf16[1,384,768]{2,1,0:T(8,128)(2,1)S(1)}, u32[]{:S(2)}, u32[]{:S(2)}) collective-permute-start(bf16[1,384,768]{2,1,0:T(8,128)(2,1)S(1)} %get-tuple-element.254), channel_id=1, source_target_pairs={{0,16},{1,17},{2,18},{3,19},{4,20},{5,21},{6,22},{7,23},{8,24},{9,... | collective-permute-start | bytes 1769480 | tf_op jit(solution)/shard_map/ppermute | solution.py:17
  196.2 100.6 %collective-permute-start.1 = (bf16[1,384,768]{2,1,0:T(8,128)(2,1)}, bf16[1,384,768]{2,1,0:T(8,128)(2,1)S(1)}, u32[]{:S(2)}, u32[]{:S(2)}) collective-permute-start(bf16[1,384,768]{2,1,0:T(8,128)(2,1)} %get-tuple-element.268), channel_id=1, source_target_pairs={{16,0},{17,1},{18,2},{19,3},{20,4},{21,5},{22,6},{23,7},{24,8},{25... | collective-permute-start | bytes 1769480 | tf_op jit(solution)/shard_map/ppermute | solution.py:17
  296.8 31.2 %copy-start.5 = (f32[384,768]{1,0:T(8,128)S(1)}, f32[384,768]{1,0:T(8,128)}, u32[]{:S(2)}) copy-start(f32[384,768]{1,0:T(8,128)} %copy-done.4) | copy-start | bytes 3538948
  296.9 31.2 %copy-start.49 = (f32[768]{0:T(1024)S(1)}, f32[768]{0:T(1024)}, u32[]{:S(2)}) copy-start(f32[768]{0:T(1024)} %copy-done.48) | copy-start | bytes 9220
  296.9 31.2 %copy-start.51 = (f32[384]{0:T(512)S(1)}, f32[384]{0:T(512)}, u32[]{:S(2)}) copy-start(f32[384]{0:T(512)} %copy-done.50) | copy-start | bytes 4612
  296.9 31.2 %copy-start.54 = (f32[384]{0:T(512)S(1)}, f32[384]{0:T(512)}, u32[]{:S(2)}) copy-start(f32[384]{0:T(512)} %copy-done.53) | copy-start | bytes 4612
  296.9 33.1 %copy-start.58 = (f32[384]{0:T(512)S(1)}, f32[384]{0:T(512)}, u32[]{:S(2)}) copy-start(f32[384]{0:T(512)} %copy-done.57) | copy-start | bytes 4612
  298.4 7.6 %copy-start.16 = (f32[1,384,3072]{2,1,0:T(8,128)S(1)}, f32[1,384,3072]{2,1,0:T(8,128)}, u32[]{:S(2)}) copy-start(f32[1,384,3072]{2,1,0:T(8,128)} %get-tuple-element.193) | copy-start | bytes 14155780 | tf_op jit(solution)/shard_map/cond
  303.3 17.4 %slice-start.12 = ((s8[4718592]{0:T(1024)(128)(4,1)}), s8[4194304]{0:T(1024)(128)(4,1)S(1)}, s32[]{:S(2)}) async-start(s8[4718592]{0:T(1024)(128)(4,1)} %bitcast.365), calls=%async_computation.13 | async-start | bytes 8388608 | tf_op jit(solution)/shard_map/cond
  306.0 14.7 %copy-start.45 = (bf16[1,384,768]{2,1,0:T(8,128)(2,1)}, bf16[1,384,768]{2,1,0:T(8,128)(2,1)S(1)}, u32[]{:S(2)}) copy-start(bf16[1,384,768]{2,1,0:T(8,128)(2,1)S(1)} %get-tuple-element.432) | copy-start | bytes 1769476 | tf_op jit(solution)/shard_map/cond
  306.0 14.7 %slice-start.13 = ((s8[4718592]{0:T(1024)(128)(4,1)}), s8[524288]{0:T(1024)(128)(4,1)S(1)}, s32[]{:S(2)}) async-start(s8[4718592]{0:T(1024)(128)(4,1)} %bitcast.365), calls=%async_computation.14 | async-start | bytes 1048576 | tf_op jit(solution)/shard_map/cond
  331.8 8.7 %slice-start = ((s8[7077888]{0:T(1024)(128)(4,1)}), s8[2883584]{0:T(1024)(128)(4,1)S(1)}, s32[]{:S(2)}) async-start(s8[7077888]{0:T(1024)(128)(4,1)} %bitcast.296), calls=%async_computation.1 | async-start | bytes 5767168
  378.7 132.4 %copy-start.1 = (f32[2,3072]{1,0:T(2,128)S(1)}, f32[2,3072]{1,0:T(2,128)}, u32[]{:S(2)}) copy-start(f32[2,3072]{1,0:T(2,128)} %param.31) | copy-start | bytes 73732
  (36 other events, 144.0 us)
Sparse Core Ops, SparseCore 0:
  374.8 121.7 all-reduce.2

commit v2 on v0

--- a/solution.py
+++ b/solution.py
@@ -1,6 +1,10 @@
+import functools
+
 import jax
 import jax.numpy as jnp
 from jax import lax
+from jax.experimental import pallas as pl
+from jax.experimental.pallas import tpu as pltpu
 from jax.sharding import PartitionSpec as P
 
 HEADS = 12
@@ -300,7 +304,7 @@
     return (grad_qk, grad_vo)
 
 
-def local(
+def local_any(
     tokens,
     segments,
     cotangent,
@@ -488,7 +492,896 @@
     )
 
 
+MESH = pl.DeviceIdType.MESH
+LOW = jnp.bfloat16
+CHIPS = 8
+FAR = 3
+MASKED = -1e30
+
+
+class Place:
+    def __init__(self):
+        self.section = lax.axis_index("section")
+        shard = lax.axis_index("dp")
+        self.core = shard % 2
+        self.chip = shard // 2
+        self.across = self.chip % 2
+        self.along = self.chip // 2
+        self.pos = self.along + self.across * (7 - 2 * self.along)
+
+    def chip_at(self, step):
+        spot = (self.pos + step + CHIPS) % CHIPS
+        across = spot // 4
+        along = spot + across * (7 - 2 * spot)
+        return along * 2 + across
+
+    def ring(self, step):
+        return (self.section, self.chip_at(step) * 2 + self.core)
+
+    def sibling(self):
+        return (self.section, self.chip * 2 + 1 - self.core)
+
+    def peer(self):
+        return (1 - self.section, self.chip * 2 + self.core)
+
+    def folds(self):
+        near = self.along + 1 - 2 * (self.along % 2)
+        far = (self.along + 2) % 4
+        return (
+            self.sibling(),
+            (self.section, (self.along * 2 + 1 - self.across) * 2 + self.core),
+            (self.section, (near * 2 + self.across) * 2 + self.core),
+            (self.section, (far * 2 + self.across) * 2 + self.core),
+            self.peer(),
+        )
+
+
+def enter(place):
+    barrier = pltpu.get_barrier_semaphore()
+    others = (place.ring(1), place.ring(-1)) + place.folds()
+    for other in others:
+        pl.semaphore_signal(barrier, inc=1, device_id=other, device_id_type=MESH)
+    pl.semaphore_wait(barrier, len(others))
+
+
+class Piece:
+    def __init__(self, ref, by_rows, low, span, slot):
+        self.ref, self.by_rows, self.low, self.span, self.slot = ref, by_rows, low, span, slot
+
+    def at(self, chip, core, half=None):
+        low, span = self.low, self.span
+        if half is not None:
+            span = span // 2
+            low = low + half * span
+        if self.by_rows:
+            return self.ref.at[chip, core, low : low + span, :]
+        return self.ref.at[chip, core, :, low : low + span]
+
+
+def piece_list(qk, vo, w_in, w_out, cross):
+    return [
+        Piece(qk, False, 0, 1536, 0),
+        Piece(vo, False, 0, 1536, 1),
+        Piece(w_in, False, 0, 1536, 2),
+        Piece(w_in, False, 1536, 1536, 3),
+        Piece(w_out, True, 0, 96, 0),
+        Piece(w_out, True, 96, 96, 1),
+        Piece(cross, False, 0, 1536, 4),
+        Piece(cross, False, 1536, 1536, 5),
+    ]
+
+
+class Gather:
+    def __init__(self, place, pieces, ring_send, ring_recv, side_send, side_recv):
+        self.place, self.pieces = place, pieces
+        self.ring_send, self.ring_recv, self.side_send, self.side_recv = ring_send, ring_recv, side_send, side_recv
+
+    def ring_copy(self, p, way, hop):
+        sign = 1 - 2 * way
+        ref = self.pieces[p].at(self.place.chip_at(-sign * hop), self.place.core, way if hop == FAR else None)
+        return pltpu.make_async_remote_copy(
+            ref, ref, self.ring_send.at[p, way, hop], self.ring_recv.at[p, way, hop],
+            device_id=self.place.ring(sign), device_id_type=MESH,
+        )
+
+    def arrival(self, p, way, hop, core):
+        sign = 1 - 2 * way
+        return self.pieces[p].at(self.place.chip_at(-sign * (hop + 1)), core, way if hop == FAR else None)
+
+    def side_copy(self, p, k, core):
+        if k == 0:
+            ref = self.pieces[p].at(self.place.chip, core)
+        else:
+            ref = self.arrival(p, (k - 1) // 4, (k - 1) % 4, core)
+        return pltpu.make_async_remote_copy(
+            ref, ref, self.side_send.at[p, k], self.side_recv.at[p, k],
+            device_id=self.place.sibling(), device_id_type=MESH,
+        )
+
+    def start(self, p):
+        self.ring_copy(p, 0, 0).start()
+        self.ring_copy(p, 1, 0).start()
+        self.side_copy(p, 0, self.place.core).start()
+
+    def event(self, p, way, hop):
+        ref = self.arrival(p, way, hop, self.place.core)
+        pltpu.make_async_remote_copy(
+            ref, ref, self.ring_send.at[p, way, hop], self.ring_recv.at[p, way, hop],
+            device_id=self.place.ring(1), device_id_type=MESH,
+        ).wait_recv()
+        if hop < FAR:
+            self.ring_copy(p, way, hop + 1).start()
+        self.side_copy(p, 1 + 4 * way + hop, self.place.core).start()
+
+    def side_arrivals(self, p):
+        for k in range(9):
+            self.side_copy(p, k, 1 - self.place.core).wait_recv()
+
+    def finish(self, p):
+        for way in range(2):
+            for hop in range(4):
+                self.ring_copy(p, way, hop).wait_send()
+        for k in range(9):
+            self.side_copy(p, k, self.place.core).wait_send()
+
+    def steps(self, pair, then):
+        found = []
+        for hop in range(4):
+            for i, p in enumerate(pair):
+                for way in range(2):
+                    found.append(functools.partial(self.event, p, way, hop))
+                if hop == 2 and i < len(then):
+                    found.append(functools.partial(self.start, then[i]))
+        return found
+
+
+class Scatter:
+    def __init__(self, place, pieces, side_c, side_r, land_c, land_r, near_c, near_r, ring_send, ring_recv, side_send, side_recv):
+        self.place, self.pieces = place, pieces
+        self.side_c, self.side_r, self.land_c, self.land_r = side_c, side_r, land_c, land_r
+        self.near_c, self.near_r = near_c, near_r
+        self.ring_send, self.ring_recv, self.side_send, self.side_recv = ring_send, ring_recv, side_send, side_recv
+
+    def cut(self, p, ref, half):
+        piece = self.pieces[p]
+        if half is None:
+            return ref
+        span = piece.span // 2
+        if piece.by_rows:
+            return ref.at[half * span : (half + 1) * span, :]
+        return ref.at[:, half * span : (half + 1) * span]
+
+    def from_side(self, p, chip, half=None):
+        piece = self.pieces[p]
+        return self.cut(p, (self.side_r if piece.by_rows else self.side_c).at[piece.slot, chip], half)
+
+    def landed(self, p, way, step, half=None):
+        piece = self.pieces[p]
+        if step == 0:
+            return (self.near_r if piece.by_rows else self.near_c).at[piece.slot, way]
+        return self.cut(p, (self.land_r if piece.by_rows else self.land_c).at[piece.slot, way, step - 1], half)
+
+    def side_copy(self, p):
+        piece = self.pieces[p]
+        span = slice(piece.low, piece.low + piece.span)
+        other = 1 - self.place.core
+        src = piece.ref.at[:, other, span, :] if piece.by_rows else piece.ref.at[:, other, :, span]
+        dst = (self.side_r if piece.by_rows else self.side_c).at[piece.slot]
+        return pltpu.make_async_remote_copy(
+            src, dst, self.side_send.at[p], self.side_recv.at[p],
+            device_id=self.place.sibling(), device_id_type=MESH,
+        )
+
+    def chip_of(self, way, step):
+        sign = 1 - 2 * way
+        return self.place.chip_at(sign * (4 - step))
+
+    def ring_copy(self, p, way, step):
+        sign = 1 - 2 * way
+        half = way if step == 0 else None
+        return pltpu.make_async_remote_copy(
+            self.pieces[p].at(self.chip_of(way, step), self.place.core, half), self.landed(p, way, step, half),
+            self.ring_send.at[p, way, step], self.ring_recv.at[p, way, step],
+            device_id=self.place.ring(sign), device_id_type=MESH,
+        )
+
+    def hand_over(self, p):
+        self.side_copy(p).start()
+
+    def start(self, p):
+        self.side_copy(p).wait_recv()
+        for way in range(2):
+            chip = self.chip_of(way, 0)
+            own = self.pieces[p].at(chip, self.place.core, way)
+            total = own[...].astype(jnp.float32) + self.from_side(p, chip, way)[...].astype(jnp.float32)
+            own[...] = total.astype(LOW)
+            self.ring_copy(p, way, 0).start()
+
+    def event(self, p, way, step):
+        self.ring_copy(p, way, step).wait_recv()
+        chip = self.chip_of(way, step + 1)
+        for half in range(2):
+            own = self.pieces[p].at(chip, self.place.core, half)
+            total = own[...].astype(jnp.float32) + self.from_side(p, chip, half)[...].astype(jnp.float32)
+            if step > 0 or half == way:
+                total = total + self.landed(p, way, step, half)[...].astype(jnp.float32)
+            own[...] = total.astype(LOW)
+        self.ring_copy(p, way, step + 1).start()
+
+    def last(self, p):
+        chip = self.place.chip
+        total = self.pieces[p].at(chip, self.place.core)[...].astype(jnp.float32)
+        total = total + self.from_side(p, chip)[...].astype(jnp.float32)
+        for way in range(2):
+            self.ring_copy(p, way, 3).wait_recv()
+            total = total + self.landed(p, way, 3)[...].astype(jnp.float32)
+        return total
+
+    def finish(self, p):
+        self.side_copy(p).wait_send()
+        for way in range(2):
+            for step in range(4):
+                self.ring_copy(p, way, step).wait_send()
+
+    def steps(self, pair, then, after):
+        found = []
+        for step in range(3):
+            for i, p in enumerate(pair):
+                for way in range(2):
+                    found.append(functools.partial(self.event, p, way, step))
+                if step == 2 and i < len(then):
+                    found.append(functools.partial(self.start, then[i]))
+        for p in pair:
+            found.append(functools.partial(after, p))
+        return found
+
+
+def serve(queue, count=None):
+    for _ in range(len(queue) if count is None else min(count, len(queue))):
+        queue.pop(0)()
+
+
+def nn(left, right):
+    return jnp.dot(left, right, preferred_element_type=jnp.float32)
+
+
+def nt(left, right):
+    return lax.dot_general(left, right, (((1,), (1,)), ((), ())), preferred_element_type=jnp.float32)
+
+
+def tn(left, right):
+    return lax.dot_general(left, right, (((0,), (0,)), ((), ())), preferred_element_type=jnp.float32)
+
+
+def tiles(low, high, body):
+    def step(j, carry):
+        body(j)
+        return carry
+
+    lax.fori_loop(low, high, step, 0)
+
+
+def span_of(j, width):
+    return pl.ds(pl.multiple_of(j * width, width), width)
+
+
+def columns_of(ref, at):
+    block = ref[:, :, :, at]
+    return block.reshape(block.shape[0] * block.shape[1] * block.shape[2], block.shape[3])
+
+
+def head_masks(length, value):
+    lane = lax.broadcasted_iota(jnp.int32, (length, 128), 1)
+    first = jnp.where(lane < 64, value, 0.0).astype(LOW)
+    second = jnp.where(lane < 64, 0.0, value).astype(LOW)
+    return first, second
+
+
+def mask_scores(bias_ref, key_row, query_row, causal):
+    length = bias_ref.shape[0]
+    keys = jnp.transpose(jnp.broadcast_to(key_row.astype(jnp.float32), (128, length)))
+    keys = jnp.concatenate([keys] * (length // 128), axis=1)
+    same = keys == jnp.broadcast_to(query_row.astype(jnp.float32), (length, length))
+    if causal:
+        key_at = lax.broadcasted_iota(jnp.int32, (length, length), 0)
+        query_at = lax.broadcasted_iota(jnp.int32, (length, length), 1)
+        same = same & (key_at <= query_at)
+    bias_ref[...] = jnp.where(same, 0.0, MASKED)
+
+
+def attend_pairs(q_ref, k_ref, v_ref, bias_ref, o_ref, lse_ref, p_ref, low, high):
+    masks = head_masks(q_ref.shape[0], 0.125)
+
+    def pair(i):
+        at = span_of(i, 128)
+        q2, k2 = q_ref[:, at], k_ref[:, at]
+        v_turned = jnp.transpose(v_ref[:, at])
+        parts = []
+        for h in range(2):
+            scores = nt(k2 * masks[h], q2) + bias_ref[...]
+            peak = jnp.max(scores, axis=0, keepdims=True)
+            exponent = jnp.exp(scores - peak)
+            summed = jnp.sum(exponent, axis=0, keepdims=True)
+            soft = (exponent * (1.0 / summed)).astype(LOW)
+            if p_ref is not None:
+                p_ref[2 * i + h] = soft
+            if lse_ref is not None:
+                lse_ref[2 * i + h] = peak + jnp.log(summed)
+            parts.append(nn(v_turned[64 * h : 64 * h + 64], soft))
+        o_ref[:, at] = jnp.transpose(jnp.concatenate(parts, axis=0)).astype(LOW)
+
+    tiles(low, high, pair)
+
+
+def attend_back_pairs(q_ref, k_ref, v_ref, bias_ref, lse_ref, p_ref, do_ref, low, high):
+    masks = head_masks(q_ref.shape[0], 0.125)
+    ones = head_masks(q_ref.shape[0], 1.0)
+
+    def pair(i):
+        at = span_of(i, 128)
+        q2, k2, v2, do2 = q_ref[:, at], k_ref[:, at], v_ref[:, at], do_ref[:, at]
+        k_turned = jnp.transpose(k2)
+        parts = []
+        dk = dv = None
+        for h in range(2):
+            if p_ref is not None:
+                low_soft = p_ref[2 * i + h]
+                soft = low_soft.astype(jnp.float32)
+            else:
+                soft = jnp.exp(nt(k2 * masks[h], q2) + bias_ref[...] - lse_ref[2 * i + h])
+                low_soft = soft.astype(LOW)
+            dv_h = nn(low_soft, do2 * ones[h])
+            d_soft = nt(v2 * ones[h], do2)
+            inner = jnp.sum(soft * d_soft, axis=0, keepdims=True)
+            d_scores = (soft * (d_soft - inner)).astype(LOW)
+            dk_h = nn(d_scores, q2 * masks[h])
+            parts.append(nn(k_turned[64 * h : 64 * h + 64], d_scores))
+            dk = dk_h if dk is None else dk + dk_h
+            dv = dv_h if dv is None else dv + dv_h
+        q_ref[:, at] = (jnp.transpose(jnp.concatenate(parts, axis=0)) * 0.125).astype(LOW)
+        k_ref[:, at] = dk.astype(LOW)
+        v_ref[:, at] = dv.astype(LOW)
+
+    tiles(low, high, pair)
+
+
+def gelu_parts(u):
+    size = jnp.abs(u)
+    bell = jnp.exp(-0.5 * u * u)
+    t = 1.0 / (1.0 + 0.2316419 * size)
+    tail = t * (0.127414796 + t * (-0.142248368 + t * (0.710706870 + t * (-0.726576013 + t * 0.530702714)))) * bell
+    upper = jnp.where(u < 0, tail, 1.0 - tail)
+    return u * upper, upper + u * bell * 0.3989422804014327
+
+
+def norm_pass(norm_ref, rstd_ref, gain, shift, hidden_ref, low_ref):
+    def rows(j):
+        at = span_of(j, 64)
+        resid = norm_ref[at, :]
+        center = resid - jnp.mean(resid, axis=-1, keepdims=True)
+        rstd = lax.rsqrt(jnp.mean(center * center, axis=-1, keepdims=True) + NORM_EPSILON)
+        normal = center * rstd
+        norm_ref[at, :] = normal
+        rstd_ref[at, :] = rstd
+        result = normal * gain + shift
+        if hidden_ref is not None:
+            hidden_ref[at, :] = result
+        low_ref[at, :] = result.astype(LOW)
+
+    tiles(0, norm_ref.shape[0] // 64, rows)
+
+
+def norm_undo(norm_ref, rstd_ref, gain, source_ref, grad_ref, low_ref):
+    width = norm_ref.shape[1]
+
+    def rows(j, carry):
+        d_gain, d_shift, d_low = carry
+        at = span_of(j, 64)
+        dy = source_ref[at, :].astype(jnp.float32)
+        normal = norm_ref[at, :]
+        scaled = dy * gain
+        mean = jnp.mean(scaled, axis=-1, keepdims=True)
+        along = jnp.mean(scaled * normal, axis=-1, keepdims=True)
+        d_resid = rstd_ref[at, :] * (scaled - mean - normal * along)
+        grad_ref[at, :] = d_resid
+        low = d_resid.astype(LOW)
+        low_ref[at, :] = low
+        return (
+            d_gain + jnp.sum(dy * normal, axis=0, keepdims=True),
+            d_shift + jnp.sum(dy, axis=0, keepdims=True),
+            d_low + jnp.sum(low.astype(jnp.float32), axis=0, keepdims=True),
+        )
+
+    zero = jnp.zeros((1, width), jnp.float32)
+    return lax.fori_loop(0, norm_ref.shape[0] // 64, rows, (zero, zero, zero))
+
+
+def column_total(ref):
+    return jnp.sum(ref[...].astype(jnp.float32), axis=0, keepdims=True)
+
+
+def layer_kernel(
+    tokens, segments, gains, biases, ffn_bias, cotangent, s_qk, s_vo, s_cqk, s_cvo, s_in, s_out,
+    out_layer, out_input, out_qk, out_vo, out_cqk, out_cvo, out_in, out_out, out_small,
+    w_qk, w_vo, w_in, w_out, w_x,
+    side_c, side_r, land_c, land_r, near_c, near_r, x_land, small, small_land,
+    sec_bias, sec_gain, sec_fbias, b1_rows,
+    q, k, v, o, h_low, norm_a, h, act, slope, norm_f, d_ffn, score_bias, x_send, x_recv,
+    qc, kc, vc, p_c, oc, h2_low, norm_c, d_branch, d_mixed, grad, lse, rstd_a, rstd_f, rstd_c,
+    load_sem, peer_send, peer_recv, rs, rr, ss, sr, rs2, rr2, ss2, sr2, fold_send, fold_recv, out_sem,
+):
+    place = Place()
+    chip, core = place.chip, place.core
+    width = tokens.shape[-1]
+    encoder, decoder = place.section == 0, place.section == 1
+    x = tokens.at[0, 0]
+    loads = [
+        pltpu.make_async_copy(src.at[0], dst.at[chip, core], load_sem.at[i])
+        for i, (src, dst) in enumerate([(s_qk, w_qk), (s_vo, w_vo), (s_in, w_in), (s_out, w_out)])
+    ]
+    for copy in loads:
+        copy.start()
+    enter(place)
+    own_cross = [
+        pltpu.make_async_copy(src.at[0], w_x.at[chip, core, :, i * width : (i + 1) * width], load_sem.at[4 + i])
+        for i, src in enumerate([s_cqk, s_cvo])
+    ]
+    from_encoder = [
+        pltpu.make_async_remote_copy(
+            src.at[0], w_x.at[chip, core, :, (2 + i) * width : (3 + i) * width], peer_send.at[i], peer_recv.at[i],
+            device_id=place.peer(), device_id_type=MESH,
+        )
+        for i, src in enumerate([s_cqk, s_cvo])
+    ]
+    pieces = piece_list(w_qk, w_vo, w_in, w_out, w_x)
+    gather = Gather(place, pieces, rs, rr, ss, sr)
+    scatter = Scatter(place, pieces, side_c, side_r, land_c, land_r, near_c, near_r, rs2, rr2, ss2, sr2)
+    for copy in loads:
+        copy.wait()
+    gather.start(0)
+    gather.start(1)
+    cot_load = pltpu.make_async_copy(cotangent, d_mixed, load_sem.at[6])
+
+    @pl.when(encoder)
+    def _():
+        for copy in from_encoder:
+            copy.start()
+        sec_bias[0:6] = biases[0:6]
+        sec_gain[0:1] = gains[0:1]
+        sec_fbias[...] = ffn_bias[0:1]
+        mask_scores(score_bias, segments[0], segments[0], False)
+
+    @pl.when(decoder)
+    def _():
+        for copy in own_cross:
+            copy.start()
+        cot_load.start()
+        sec_bias[0:6] = biases[6:12]
+        sec_gain[0:1] = gains[2:3]
+        sec_fbias[...] = ffn_bias[1:2]
+        mask_scores(score_bias, segments[1], segments[1], True)
+
+    small[...] = jnp.zeros_like(small)
+    shared = gather.steps((0, 1), (2, 3))
+    serve(shared)
+    gather.side_arrivals(0)
+    gather.side_arrivals(1)
+    shared = gather.steps((2, 3), (4, 5))
+
+    def project(j):
+        at = span_of(j, 256)
+        past = pl.ds(pl.multiple_of(width + j * 256, 256), 256)
+        q[:, at] = (nn(x[...], columns_of(w_qk, at)) + sec_bias[0:1, at]).astype(LOW)
+        k[:, at] = nn(x[...], columns_of(w_qk, past)).astype(LOW)
+        v[:, at] = (nn(x[...], columns_of(w_vo, at)) + sec_bias[1:2, at]).astype(LOW)
+
+    tiles(0, 3, project)
+    serve(shared, 4)
+    attend_pairs(q, k, v, score_bias, o, lse, None, 0, 3)
+    serve(shared, 2)
+    attend_pairs(q, k, v, score_bias, o, lse, None, 3, 6)
+    serve(shared, 2)
+
+    def self_out(j):
+        at = span_of(j, 256)
+        past = pl.ds(pl.multiple_of(width + j * 256, 256), 256)
+        norm_a[:, at] = x[:, at].astype(jnp.float32) + nn(o[...], columns_of(w_vo, past)) + sec_bias[2:3, at]
+
+    tiles(0, 3, self_out)
+    norm_pass(norm_a, rstd_a, sec_gain[0:1], sec_bias[3:4], h, h_low)
+
+    def ffn_up(low_ref, low, high):
+        def tile(j):
+            at = span_of(j, 256)
+            u = nn(low_ref[...], columns_of(w_in, at)) + sec_fbias[:, at]
+            value, rise = gelu_parts(u)
+            act[:, at] = value.astype(LOW)
+            slope[:, at] = rise.astype(LOW)
+
+        tiles(low, high, tile)
+
+    def ffn_down():
+        def tile(j):
+            at = span_of(j, 256)
+            norm_f[:, at] = h[:, at] + nn(act[...], columns_of(w_out, at)) + sec_bias[4:5, at]
+
+        tiles(0, 3, tile)
+
+    def ffn_slope():
+        def tile(j):
+            at = span_of(j, width)
+            block = w_out[pl.ds(2 * j, 2)].reshape(width, width)
+            d_pre = (nt(d_ffn[...], block) * slope[:, at].astype(jnp.float32)).astype(LOW)
+            slope[:, at] = d_pre
+            b1_rows[j] = jnp.sum(d_pre.astype(jnp.float32), axis=0, keepdims=True)
+
+        tiles(0, 4, tile)
+
+    def ffn_hidden():
+        def tile(j):
+            at = span_of(j, width)
+            grad[...] += nt(slope[:, at], columns_of(w_in, at))
+
+        tiles(0, 4, tile)
+
+    def grad_w_out():
+        def tile(c):
+            block = tn(act[:, span_of(c, 384)], d_ffn[...])
+            w_out[c] = block.astype(LOW).reshape(2, 192, width)
+
+        tiles(0, CHIPS, tile)
+
+    def store(ref, at, value):
+        ref[:, :, :, at] = value.astype(LOW).reshape(CHIPS, 2, 48, value.shape[1])
+
+    def grad_w_in(low_ref):
+        def tile(j):
+            at = span_of(j, width)
+            store(w_in, at, tn(low_ref[...], slope[:, at]))
+
+        tiles(0, 4, tile)
+
+    def set_small(row, value):
+        small[row : row + 1, :] = value
+
+    def set_b1(section):
+        for j in range(4):
+            set_small(21 + 4 * section + j, b1_rows[j])
+
+    def self_back_a(section):
+        gain, shift, branch = norm_undo(norm_a, rstd_a, sec_gain[0:1], grad, grad, d_branch)
+        set_small(2 * section, gain)
+        set_small(5 + 6 * section + 3, shift)
+        set_small(5 + 6 * section + 2, branch)
+        d_mixed[...] = nt(d_branch[...], columns_of(w_vo, slice(width, 2 * width))).astype(LOW)
+
+    def self_back_b(section):
+        set_small(5 + 6 * section, column_total(q))
+        set_small(5 + 6 * section + 1, column_total(v))
+        grad[...] += nt(q[...], columns_of(w_qk, slice(0, width)))
+        grad[...] += nt(k[...], columns_of(w_qk, slice(width, 2 * width)))
+        grad[...] += nt(v[...], columns_of(w_vo, slice(0, width)))
+        pltpu.make_async_copy(grad, out_input.at[0, 0], out_sem.at[1]).start()
+
+    def self_back_qk():
+        store(w_qk, slice(0, width), tn(x[...], q[...]))
+        store(w_qk, slice(width, 2 * width), tn(x[...], k[...]))
+
+    def self_back_vo():
+        store(w_vo, slice(0, width), tn(x[...], v[...]))
+        store(w_vo, slice(width, 2 * width), tn(o[...], d_branch[...]))
+
+    def result_at(p):
+        holder = norm_f if p < 4 else norm_c
+        return holder.at[96 * (p % 4) : 96 * (p % 4) + 96, :]
+
+    def out_copies(p, half):
+        source = result_at(p)
+        if p in (4, 5):
+            return pltpu.make_async_copy(
+                source.at[48 * half : 48 * half + 48],
+                out_out.at[0, 96 * (p - 4) + 48 * half : 96 * (p - 4) + 48 * half + 48, :],
+                out_sem.at[2 + 2 * p + half],
+            )
+        target, first = {0: (out_qk, 0), 1: (out_vo, 0), 2: (out_in, 0), 3: (out_in, 1536)}[p] if p < 4 else (
+            (out_cqk, out_cvo)[half], -width * half
+        )
+        low = first + width * half
+        if p == 7:
+            source = x_land
+        return pltpu.make_async_copy(
+            source.at[48 * half : 48 * half + 48], target.at[0, :, low : low + width], out_sem.at[2 + 2 * min(p, 6) + half]
+        )
+
+    def finish_piece(p):
+        total = scatter.last(p)
+        target = result_at(p)
+        if p in (4, 5):
+            target[...] = total
+        else:
+            target[0:48] = total[:, :width]
+            target[48:96] = total[:, width:]
+        if p == 7:
+            to_encoder.start()
+        else:
+            out_copies(p, 0).start()
+            out_copies(p, 1).start()
+
+    to_encoder = pltpu.make_async_remote_copy(
+        result_at(7), x_land, peer_send.at[3], peer_recv.at[3], device_id=place.peer(), device_id_type=MESH
+    )
+    cross_copy = pltpu.make_async_remote_copy(
+        x_send, x_recv, peer_send.at[2], peer_recv.at[2], device_id=place.peer(), device_id_type=MESH
+    )
+    layer_copy = pltpu.make_async_copy(x_send, out_layer.at[0, 0], out_sem.at[0])
+
+    def fold(i):
+        return pltpu.make_async_remote_copy(
+            small, small_land.at[i], fold_send.at[i], fold_recv.at[i], device_id=place.folds()[i], device_id_type=MESH
+        )
+
+    def fold_start(i):
+        fold(i).start()
+
+    def fold_end(i):
+        fold(i).wait()
+        small[...] = small[...] + small_land[i]
+        if i < 4:
+            fold(i + 1).start()
+
+    @pl.when(encoder)
+    def _():
+        queue = list(shared) + gather.steps((4, 5), ())
+        serve(queue, len(shared))
+        gather.side_arrivals(2)
+        gather.side_arrivals(3)
+        for part in range(4):
+            ffn_up(h_low, 3 * part, 3 * part + 3)
+            serve(queue, 4 if part < 3 else None)
+        gather.side_arrivals(4)
+        gather.side_arrivals(5)
+        ffn_down()
+        norm_pass(norm_f, rstd_f, gains[1:2], biases[5:6], None, x_send)
+        cross_copy.start()
+        layer_copy.start()
+        for copy in from_encoder:
+            copy.wait_send()
+        for p in range(6):
+            gather.finish(p)
+        layer_copy.wait()
+        cross_copy.wait()
+
+        gain, shift, branch = norm_undo(norm_f, rstd_f, gains[1:2], x_recv, grad, d_ffn)
+        set_small(1, gain)
+        set_small(5 + 5, shift)
+        set_small(5 + 4, branch)
+        ffn_slope()
+        grad_w_out()
+        scatter.hand_over(4)
+        scatter.hand_over(5)
+        ffn_hidden()
+        scatter.start(4)
+        scatter.start(5)
+        grad_w_in(h_low)
+        scatter.hand_over(2)
+        scatter.hand_over(3)
+        set_b1(0)
+        queue = scatter.steps((4, 5), (2, 3), finish_piece)
+        serve(queue, 2)
+        self_back_a(0)
+        serve(queue, 2)
+        attend_back_pairs(q, k, v, score_bias, lse, None, d_mixed, 0, 3)
+        serve(queue, 4)
+        attend_back_pairs(q, k, v, score_bias, lse, None, d_mixed, 3, 6)
+        serve(queue, 4)
+        self_back_b(0)
+        fold_start(0)
+        serve(queue)
+        queue = scatter.steps((2, 3), (0, 1), finish_piece)
+        self_back_qk()
+        scatter.hand_over(0)
+        self_back_vo()
+        scatter.hand_over(1)
+        fold_end(0)
+        serve(queue, 4)
+        fold_end(1)
+        serve(queue, 4)
+        fold_end(2)
+        serve(queue)
+        fold_end(3)
+        serve(scatter.steps((0, 1), (), finish_piece))
+        to_encoder.wait_recv()
+        out_copies(7, 0).start()
+        out_copies(7, 1).start()
+
+    @pl.when(decoder)
+    def _():
+        for copy in own_cross:
+            copy.wait()
+        for copy in from_encoder:
+            copy.wait_recv()
+        queue = list(shared) + gather.steps((4, 5), (6, 7)) + gather.steps((6, 7), ())
+        serve(queue)
+        for p in range(2, 8):
+            gather.side_arrivals(p)
+        mask_scores(score_bias, segments[0], segments[1], False)
+
+        def cross_query(j):
+            at = span_of(j, 256)
+            qc[:, at] = (nn(h_low[...], columns_of(w_x, at)) + biases[12:13, at]).astype(LOW)
+
+        tiles(0, 3, cross_query)
+        cross_copy.wait_recv()
+
+        def cross_keys(j):
+            at = span_of(j, 256)
+            key_at = pl.ds(pl.multiple_of(2 * width + j * 256, 256), 256)
+            value_at = pl.ds(pl.multiple_of(3 * width + j * 256, 256), 256)
+            kc[:, at] = nn(x_recv[...], columns_of(w_x, key_at)).astype(LOW)
+            vc[:, at] = (nn(x_recv[...], columns_of(w_x, value_at)) + biases[13:14, at]).astype(LOW)
+
+        tiles(0, 3, cross_keys)
+        attend_pairs(qc, kc, vc, score_bias, oc, None, p_c, 0, 6)
+
+        def cross_out(j):
+            at = span_of(j, 256)
+            past = pl.ds(pl.multiple_of(width + j * 256, 256), 256)
+            norm_c[:, at] = h[:, at] + nn(oc[...], columns_of(w_x, past)) + biases[14:15, at]
+
+        tiles(0, 3, cross_out)
+        norm_pass(norm_c, rstd_c, gains[4:5], biases[15:16], h, h2_low)
+        ffn_up(h2_low, 0, 12)
+        ffn_down()
+        norm_pass(norm_f, rstd_f, gains[3:4], biases[11:12], None, x_send)
+        layer_copy.start()
+        cot_load.wait()
+        gain, shift, branch = norm_undo(norm_f, rstd_f, gains[3:4], d_mixed, grad, d_ffn)
+        set_small(3, gain)
+        set_small(5 + 11, shift)
+        set_small(5 + 10, branch)
+        ffn_slope()
+        ffn_hidden()
+        gain, shift, branch = norm_undo(norm_c, rstd_c, gains[4:5], grad, grad, d_branch)
+        set_small(4, gain)
+        set_small(5 + 15, shift)
+        set_small(5 + 14, branch)
+        d_mixed[...] = nt(d_branch[...], columns_of(w_x, slice(width, 2 * width))).astype(LOW)
+        attend_back_pairs(qc, kc, vc, None, None, p_c, d_mixed, 0, 6)
+        layer_copy.wait()
+        x_send[...] = (
+            nt(kc[...], columns_of(w_x, slice(2 * width, 3 * width)))
+            + nt(vc[...], columns_of(w_x, slice(3 * width, 4 * width)))
+        ).astype(LOW)
+        cross_copy.start()
+        for p in range(8):
+            gather.finish(p)
+        grad_w_out()
+        scatter.hand_over(4)
+        scatter.hand_over(5)
+        grad_w_in(h2_low)
+        scatter.hand_over(2)
+        scatter.hand_over(3)
+        scatter.start(4)
+        scatter.start(5)
+        grad[...] += nt(qc[...], columns_of(w_x, slice(0, width)))
+        store(w_x, slice(2 * width, 3 * width), tn(x_recv[...], kc[...]))
+        store(w_x, slice(3 * width, 4 * width), tn(x_recv[...], vc[...]))
+        scatter.hand_over(7)
+        queue = scatter.steps((4, 5), (7, 6), finish_piece)
+        serve(queue, 4)
+        store(w_x, slice(0, width), tn(h_low[...], qc[...]))
+        store(w_x, slice(width, 2 * width), tn(oc[...], d_branch[...]))
+        scatter.hand_over(6)
+        serve(queue, 4)
+        set_b1(1)
+        set_small(5 + 12, column_total(qc))
+        set_small(5 + 13, column_total(vc))
+        mask_scores(score_bias, segments[1], segments[1], True)
+        self_back_a(1)
+        serve(queue)
+        queue = scatter.steps((7, 6), (2, 3), finish_piece)
+        attend_back_pairs(q, k, v, score_bias, lse, None, d_mixed, 0, 3)
+        serve(queue, 4)
+        attend_back_pairs(q, k, v, score_bias, lse, None, d_mixed, 3, 6)
+        serve(queue, 4)
+        self_back_b(1)
+        fold_start(0)
+        serve(queue)
+        queue = scatter.steps((2, 3), (0, 1), finish_piece)
+        self_back_qk()
+        scatter.hand_over(0)
+        self_back_vo()
+        scatter.hand_over(1)
+        fold_end(0)
+        serve(queue, 4)
+        fold_end(1)
+        serve(queue, 4)
+        fold_end(2)
+        serve(queue)
+        fold_end(3)
+        serve(scatter.steps((0, 1), (), finish_piece))
+        cross_copy.wait_send()
+        to_encoder.wait_send()
+        for p in (6, 7):
+            scatter.finish(p)
+
+    fold_end(4)
+    out_small[...] = small[...]
+    for p in range(6):
+        scatter.finish(p)
+    for p in range(7):
+        for half in range(2):
+            out_copies(p, half).wait()
+    pltpu.make_async_copy(grad, out_input.at[0, 0], out_sem.at[1]).wait()
+
+
+def layer_call(tokens, segments, cotangent, attn_qk, attn_vo, cross_qk, cross_vo, ffn_in, ffn_out, gains, biases, ffn_bias):
+    length, width = tokens.shape[2:]
+    hidden = ffn_in.shape[2]
+
+    def result(like, kind):
+        return jax.ShapeDtypeStruct(like.shape, kind)
+
+    def low(*shape):
+        return pltpu.VMEM(shape, LOW)
+
+    def full(*shape):
+        return pltpu.VMEM(shape, jnp.float32)
+
+    any_space = pl.BlockSpec(memory_space=pl.ANY)
+    in_vmem = pl.BlockSpec(memory_space=pltpu.VMEM)
+    flat, wide, exact = low(length, width), low(length, hidden), full(length, width)
+    dma = pltpu.SemaphoreType.DMA
+    scratch = [
+        low(CHIPS, 2, 48, 2 * width), low(CHIPS, 2, 48, 2 * width), low(CHIPS, 2, 48, hidden),
+        low(CHIPS, 2, 192, width), low(CHIPS, 2, 48, 4 * width),
+        low(6, CHIPS, 48, 2 * width), low(2, CHIPS, 96, width),
+        low(6, 2, 3, 48, 2 * width), low(2, 2, 3, 96, width),
+        low(6, 2, 48, width), low(2, 2, 48, width),
+        full(96, width), full(32, width), full(5, 32, width),
+        full(8, width), full(1, width), full(1, hidden), full(4, 1, width),
+        flat, flat, flat, flat, flat, exact, exact, wide, wide, exact, flat, full(length, length), flat, flat,
+        flat, flat, flat, low(HEADS, length, length), flat, flat, exact, flat, flat, exact,
+        full(HEADS, 1, length), full(length, 1), full(length, 1), full(length, 1),
+        dma((7,)), dma((4,)), dma((4,)),
+        dma((8, 2, 4)), dma((8, 2, 4)), dma((8, 9)), dma((8, 9)),
+        dma((8, 2, 4)), dma((8, 2, 4)), dma((8,)), dma((8,)),
+        dma((5,)), dma((5,)), dma((16,)),
+    ]
+    return pl.pallas_call(
+        layer_kernel,
+        out_shape=(
+            result(tokens, LOW), result(tokens, jnp.float32),
+            result(attn_qk, jnp.float32), result(attn_vo, jnp.float32),
+            result(cross_qk, jnp.float32), result(cross_vo, jnp.float32),
+            result(ffn_in, jnp.float32), result(ffn_out, jnp.float32),
+            jax.ShapeDtypeStruct((32, width), jnp.float32),
+        ),
+        in_specs=[in_vmem] * 5 + [any_space] * 7,
+        out_specs=(any_space,) * 8 + (in_vmem,),
+        scratch_shapes=scratch,
+        compiler_params=pltpu.CompilerParams(
+            collective_id=0, has_side_effects=True, vmem_limit_bytes=63 * 1024 * 1024
+        ),
+        name="layer_pair",
+    )(
+        tokens, segments, gains, biases, ffn_bias, cotangent[0],
+        attn_qk, attn_vo, cross_qk, cross_vo, ffn_in, ffn_out,
+    )
+
+
+def local_ring(
+    tokens, segments, cotangent, attn_qk, attn_vo, cross_qk, cross_vo, ffn_in, ffn_out, gains, biases, ffn_bias
+):
+    results = layer_call(
+        tokens, segments, cotangent, attn_qk, attn_vo, cross_qk, cross_vo, ffn_in, ffn_out, gains, biases, ffn_bias
+    )
+    small = results[8]
+    return results[:8] + (small[0:5], small[5:21], small[21:29].reshape(ffn_bias.shape))
+
+
 def solution(mesh):
+    any_size = mesh.shape["section"] != 2 or mesh.shape["dp"] != 2 * CHIPS
     placed = (
         P("section", "dp", None, None),
         P(None, "dp", None),
@@ -504,7 +1397,7 @@
         P(),
     )
     return jax.shard_map(
-        local,
+        local_any if any_size else local_ring,
         mesh=mesh,
         in_specs=placed,
         out_specs=(

time: 1250 us -> 280 us (0.22)
  waiting for transfers between devices: 1010 us -> 0 us
  Pallas kernels: 0 us -> 264 us
  matrix products: 99 us -> 0 us
  local copies, waits for them, and re-layouts: 76.3 us -> 11.8 us
  other arithmetic: 27.6 us -> 0 us
  between operations: 15.9 us -> 0.9 us
    reduce_scatter x4 -> x0, waiting for transfers between devices: 366 us -> none  [the longest x1 116 us: local(): lax.psum_scatter(grad_in[None], 'dp', scatter_dimension=1, tiled=True)]
    pallas_call x0 -> x1, Pallas kernels: none -> 264 us  [layer_call(): pl.pallas_call(layer_kernel, out_shape=(result(tokens, LOW), result(token...]
    all_gather x6 -> x0, waiting for transfers between devices: 256 us -> none  [the longest x1 54.5 us: local(): lax.all_gather(ffn_in, 'dp', axis=1, tiled=True)]
    unnamed x13 -> x0, waiting for transfers between devices: 154 us -> none
    psum x1 -> x0, waiting for transfers between devices: 127 us -> none  [local(): lax.psum((grad_gains, grad_biases, grad_fbias), ('section', 'dp'))]
    ppermute x4 -> x0, waiting for transfers between devices: 106 us -> none  [from_behind(): return lax.ppermute(x, axis, pairs)]
    dot_general x28 -> x0, matrix products: 99 us -> none  [the longest x8 31.2 us: product(): jnp.einsum('rld,de->rle', left, right, preferred_element_type=jnp.float32)]
    broadcast_in_dim x4 -> x0, local copies, waits for them, and re-layouts: 24.6 us -> none  [the longest x1 12.3 us: local(): grad_qk[None]]
  transfers between devices with their start and end apart: 16 -> 0, of which waited for: 16 -> 0; matrix products, arithmetic and copies ran while one was open for 4% -> 0% of each run, Pallas kernels for 0% -> 0%
where the time goes in v2:
time: 280 us; the launch traced here: 277 us
  Pallas kernels  264 us (94%)
  local copies, waits for them, and re-layouts  11.8 us (4%)
    pallas_call x1, Pallas kernels, layer_call(): pl.pallas_call(layer_kernel, out_shape=(result(tokens, LOW), result(token...  264 us
    unnamed x22, local copies, waits for them, and re-layouts  7.44 us

profile of v2, /device:TPU:0, one launch (start us, length us, event | category | flops | bytes accessed | tf_op | source)
XLA Modules:
  0.0 277.0 jit_solution(18099346413356945441)
XLA Ops:
  0.6 264.3 %layer_pair.1 = (bf16[1,1,384,768]{3,2,1,0:T(8,128)(2,1)}, f32[1,1,384,768]{3,2,1,0:T(8,128)}, f32[1,48,1536]{2,1,0:T(8,128)}, f32[1,48,1536]{2,1,0:T(8,128)}, f...) custom-call(bf16[1,1,384,768]{3,2,1,0:T(8,128)(2,1)} %tokens.1, ...), custom_call_target="tpu_custom_call" | custom-call | tf_op jit(solution)/shard_map/layer_pair/pallas_call | solution.py:1351
  265.0 0.0 copy-start
  265.0 0.9 slice.11
  265.9 0.6 reshape.25
  266.5 1.3 slice.9
  267.9 1.5 slice.10
  269.4 1.9 copy.31
  271.3 0.0 copy-done
  271.3 0.0 copy-start.4
  271.3 0.0 copy-start.3
  271.3 1.0 copy.32
  272.3 0.1 copy-done.4
  272.4 0.0 copy-start.6
  272.4 0.7 copy.33
  273.1 0.0 copy-done.3
  273.1 0.7 copy.34
  273.9 0.0 copy-done.6
  273.9 0.7 copy.35
  274.5 0.0 copy-done.5
  274.5 0.7 copy.36
  275.2 0.0 copy-done.2
  275.2 0.8 copy.37
  276.0 0.0 copy-done.1
  276.0 0.8 copy.38
  (3 shorter events, 0.0 us)
Async XLA Ops:
  265.0 6.3 %copy-start = (f32[1,1,384,768]{3,2,1,0:T(8,128)S(1)}, f32[1,1,384,768]{3,2,1,0:T(8,128)}, u32[]{:S(2)}) copy-start(f32[1,1,384,768]{3,2,1,0:T(8,128)} %get-tuple-element.41) | copy-start | bytes 3538948
  271.3 1.1 copy-start.4
  271.3 1.8 copy-start.3
  272.4 1.4 copy-start.6
  272.4 2.1 copy-start.5
  272.4 2.8 copy-start.2
  273.1 2.9 %copy-start.1 = (f32[1,192,768]{2,1,0:T(8,128)S(1)}, f32[1,192,768]{2,1,0:T(8,128)}, u32[]{:S(2)}) copy-start(f32[1,192,768]{2,1,0:T(8,128)} %get-tuple-element.47) | copy-start | bytes 1769476
